TPU v7x, 32 devices: a whole 2x2x4 slice. The times are simulated.
32 devices in a mesh: section: 2 (over core), dp: 4 (over z), seq: 4 (over y, x).
Axes of the slice: x: 2, y: 2, z: 4, core: 2. Of those that a mesh axis runs over, the one named last changes fastest.
Arguments:
- inputs: bfloat16 [8, 4096, 512], P('dp', 'seq'), may hold values from -8 to 8
- mask: int32 [8, 4096], P('dp', 'seq'), may hold values from 0 to 1, as said below
- norm_gain: float32 [2, 512], P('section'), may hold values from 0.5 to 1.5
- norm_bias: float32 [2, 512], P('section'), may hold values from -3 to 3
- nu_log: float32 [2, 256], P('section'), as said below
- theta_log: float32 [2, 256], P('section'), may hold values from -4.6 to -0.7
- w_in: bfloat16 [2, 512, 512], P('section'), may hold values from -0.1875 to 0.1875
- w_out: bfloat16 [2, 512, 512], P('section'), may hold values from -0.25 to 0.25
- skip_gain: float32 [2, 512], P('section'), may hold values from -3 to 3
- w_glu: bfloat16 [2, 512, 1024], P('section'), may hold values from -0.25 to 0.25
- b_glu: float32 [2, 1024], P('section'), may hold values from -2 to 2
- cotangent: bfloat16 [8, 4096, 512], P('dp', 'seq'), may hold values from -6 to 6
Outputs:
- activations: bfloat16 [2, 8, 4096, 512], P('section', 'dp', 'seq')
- input_grads: float32 [2, 8, 4096, 512], P('section', 'dp', 'seq')
- grad_norm_gain: float32 [2, 512], P('section')
- grad_norm_bias: float32 [2, 512], P('section')
- grad_nu_log: float32 [2, 256], P('section')
- grad_theta_log: float32 [2, 256], P('section')
- grad_w_in: float32 [2, 512, 512], P('section')
- grad_w_out: float32 [2, 512, 512], P('section')
- grad_skip_gain: float32 [2, 512], P('section')
- grad_w_glu: float32 [2, 512, 1024], P('section')
- grad_b_glu: float32 [2, 1024], P('section')
Inputs may be any that keep to these rules, and one draw needn't show every extreme that they name: `mask`: each sequence is 1 on a prefix of at least 1024 steps and 0 after it; in each aligned group of 1 sequence one is 1 on more than 3072 steps. exp(nu_log) lies between 0.1 / 4096 and 1 / 30.
All inputs are finite; a program needn't handle non-finite values.
Results may differ from a plain program's by a relative error of at most 0.015.
Values may be sent and summed in bfloat16 or wider, within the bound.
A program may use at most 192 MiB of HBM per device.

v0:
```python
import functools
import math
import types

import jax
import jax.numpy as jnp
from jax import lax
from jax.experimental import pallas as pl
from jax.experimental.pallas import tpu as pltpu
from jax.sharding import PartitionSpec as P

D = 512
STATES = 256
MICRO = 2
EPS = 1e-05
LANES = 128
ROWS = 256
SEG = 32
GLU, OUT, IN = 0, 1, 2
GRAD_ROWS = (4096, 2048, 2048)
GRAD_AT = (0, 4096, 6144)
ALL_ROWS = 8192
ROOT = math.sqrt(2.0 / math.pi)
CUBE = 0.044715

F32 = jnp.float32
BF16 = jnp.bfloat16
MESH = pl.DeviceIdType.MESH


def mm(a, b):
    return lax.dot_general(a, b, (((1,), (0,)), ((), ())), preferred_element_type=F32)


def mm_t(a, b):
    return lax.dot_general(a, b, (((1,), (1,)), ((), ())), preferred_element_type=F32)


def t_mm(a, b):
    return lax.dot_general(a, b, (((0,), (0,)), ((), ())), preferred_element_type=F32)


def complex_mul(ar, ai, br, bi):
    return ar * br - ai * bi, ar * bi + ai * br


def power(re, im, n):
    out = None
    while n:
        if n & 1:
            out = (re, im) if out is None else complex_mul(*out, re, im)
        n >>= 1
        if n:
            re, im = complex_mul(re, im, re, im)
    return out


def as_row(four):
    return jnp.concatenate([four[c : c + 1] for c in range(4)], axis=1)


def wide(tile):
    return jnp.concatenate([tile] * 4, axis=1)


def column_sum(x):
    return jnp.sum(x, axis=0, keepdims=True)


def kernel(ns, nd, per, span, names, *refs):
    r = types.SimpleNamespace(**dict(zip(names, refs)))
    tokens = per * span
    segs = tokens // SEG
    nseg = span // SEG
    tiles = tokens // ROWS
    peers = ns * nd
    s = lax.axis_index("section")
    d = lax.axis_index("dp")
    q = lax.axis_index("seq")
    other = 1 - s
    me = d * ns + q
    sibling = {"section": other}

    def seq_peer(k):
        return {"seq": lax.rem(q + k, ns)}

    def dp_peer(k):
        return {"dp": lax.rem(d + k, nd)}

    def any_peer(k):
        at = lax.rem(me + k, peers)
        return {"dp": at // ns, "seq": lax.rem(at, ns)}

    def remote(src, dst, send, recv, device):
        return pltpu.make_async_remote_copy(
            src_ref=src, dst_ref=dst, send_sem=send, recv_sem=recv, device_id=device, device_id_type=MESH
        )

    def over(low, high, body):
        lax.fori_loop(low, high, lambda k, c: (body(k), c)[1], 0)

    def row_tiles(body, init):
        def step(i, carry):
            return body(pl.ds(pl.multiple_of(i * ROWS, ROWS), ROWS), carry)

        return lax.fori_loop(0, tiles, step, init)

    barrier = pltpu.get_barrier_semaphore()

    def greet(device):
        pl.semaphore_signal(barrier, inc=1, device_id=device, device_id_type=MESH)

    greet(sibling)
    over(1, peers, lambda k: greet(any_peer(k)))
    over(1, ns, lambda k: greet({"section": other, "seq": lax.rem(q + k, ns)}))

    load_x = pltpu.make_async_copy(r.x.at[s], r.act.at[0], r.local.at[0])
    load_x.start()
    load_cot = pltpu.make_async_copy(r.cot.at[s], r.cotv, r.local.at[1])
    weights = ((r.w_in, r.win), (r.w_out, r.wout), (r.w_glu, r.wglu))
    load_w = [
        pltpu.make_async_copy(src.at[0], dst.at[s], r.local.at[2 + i]) for i, (src, dst) in enumerate(weights)
    ]
    for copy in load_w:
        copy.start()
    load_cot.start()

    rate = jnp.exp(r.nu[...])
    phase = jnp.exp(r.theta[...])
    size = jnp.exp(-rate)
    decay_re = size * jnp.cos(phase)
    decay_im = size * jnp.sin(phase)
    double = 2.0 * rate
    scale_sq = double * (
        1.0
        - double / 2.0 * (1.0 - double / 3.0 * (1.0 - double / 4.0 * (1.0 - double / 5.0 * (1.0 - double / 6.0))))
    )
    scale = jnp.sqrt(scale_sq)
    r.prm[s, 0:1, :] = r.gain[...]
    r.prm[s, 1:2, :] = r.bias[...]
    r.prm[s, 2:3, :] = r.skip[...]
    r.prm[s, 3:4, :] = r.bglu[:, :D]
    r.prm[s, 4:5, :] = r.bglu[:, D:]
    r.prm[s, 5:6, :] = jnp.concatenate([decay_re, decay_im], axis=1)
    r.prm[s, 6:7, :] = jnp.concatenate([scale, scale], axis=1)
    r.prm[s, 7:8, :] = jnp.zeros((1, D), F32)

    count = jnp.zeros((1, 1), F32)
    steps = lax.broadcasted_iota(jnp.int32, (span, LANES), 0)
    for i in range(per):
        here = jnp.sum(r.mask[pl.ds(s * per + i, 1), :], axis=1, keepdims=True)
        r.live[i * span : (i + 1) * span, :] = jnp.where(steps < here, 1.0, 0.0)
        count = count + here.astype(F32)
    count_row = jnp.broadcast_to(count, (1, LANES))
    load_x.wait()

    def mask_input(rows, total):
        x = r.act[0, rows, :].astype(F32) * wide(r.live[rows, :])
        r.act[0, rows, :] = x.astype(BF16)
        return total + column_sum(x)

    def centred(b, mean):
        def tile(rows, total):
            off = (r.act[b, rows, :].astype(F32) - mean) * wide(r.live[rows, :])
            return total + column_sum(off * off)

        return row_tiles(tile, jnp.zeros((1, D), F32))

    def put_rows(ph, upper, lower):
        for c in range(4):
            r.bnb[ph, me, c : c + 1, :] = upper[:, c * LANES : (c + 1) * LANES]
            r.bnb[ph, me, 4 + c : 5 + c, :] = lower[:, c * LANES : (c + 1) * LANES]
        r.bnb[ph, me, 8:9, :] = count_row

    def to_all(ph, k):
        block = r.bnb.at[ph, me]
        return remote(block, block, r.bn_send.at[ph, k], r.bn_recv.at[ph, k], any_peer(k))

    def send_all(ph):
        over(1, peers, lambda k: to_all(ph, k).start())

    def wait_all(ph):
        over(1, peers, lambda k: to_all(ph, k).wait_recv())

    def norm_sums(b, total):
        mean = total / jnp.maximum(wide(count_row), 1.0)
        put_rows(b, mean, centred(b, mean))

    def norm_merge(b):
        wait_all(b)
        got = r.bnb[b]
        means, spreads, counts = got[:, 0:4, :], got[:, 4:8, :], got[:, 8:9, :]
        valid = jnp.sum(counts, axis=0)
        mean = jnp.sum(counts * means, axis=0) / valid
        apart = means - mean[None]
        spread = jnp.sum(spreads + counts * apart * apart, axis=0)
        r.stat[b, 0:1, :] = as_row(mean)
        r.stat[b, 1:2, :] = as_row(lax.rsqrt(spread / valid + EPS))
        r.stat[b, 2:3, :] = wide(valid)

    norm_sums(0, row_tiles(mask_input, jnp.zeros((1, D), F32)))

    pl.semaphore_wait(barrier, peers + ns - 1)
    send_all(0)
    send_prm = remote(r.prm.at[s], r.prm.at[s], r.far_send.at[0], r.far_recv.at[0], sibling)
    send_prm.start()
    send_w = [
        remote(src.at[0], dst.at[s], r.far_send.at[1 + i], r.far_recv.at[1 + i], sibling)
        for i, (src, dst) in enumerate(weights)
    ]
    for copy in send_w:
        copy.start()

    def decay(b, sign):
        out = []
        for c in range(2):
            re = r.prm[b, 5:6, c * LANES : (c + 1) * LANES]
            im = r.prm[b, 5:6, STATES + c * LANES : STATES + (c + 1) * LANES]
            out.append((re, sign * im))
        return out

    def every(l):
        return pl.ds(l, segs, stride=SEG)

    def advance(a, state, drive):
        return (
            a[0] * state[0] - a[1] * state[1] + drive[0],
            a[1] * state[0] + a[0] * state[1] + drive[1],
        )

    place = lax.rem(lax.broadcasted_iota(jnp.int32, (segs, LANES), 0), nseg)
    owner = lax.broadcasted_iota(jnp.int32, (segs, LANES), 0) // nseg

    def moved(x, k, reverse):
        if reverse:
            return jnp.where(place < nseg - k, pltpu.roll(x, segs - k, 0), 0.0)
        return jnp.where(place >= k, pltpu.roll(x, k, 0), 0.0)

    def seg_scan(re, im, jump, reverse):
        k = 1
        while k < nseg:
            add_re, add_im = complex_mul(*jump, moved(re, k, reverse), moved(im, k, reverse))
            re, im = re + add_re, im + add_im
            jump = complex_mul(*jump, *jump)
            k *= 2
        return re, im

    def to_seq(ph, k):
        block = r.scb.at[ph, q]
        return remote(block, block, r.sc_send.at[ph, k], r.sc_recv.at[ph, k], seq_peer(k))

    def carry(ph, drive, a, reverse, between):
        def step(i, states):
            l = SEG - 1 - i if reverse else i
            return tuple(
                advance(a[c], states[c], (drive[c, every(l), :], drive[2 + c, every(l), :])) for c in range(2)
            )

        zero = jnp.zeros((segs, LANES), F32)
        ends = lax.fori_loop(0, SEG, step, ((zero, zero), (zero, zero)), unroll=4)
        jumps = [power(*a[c], SEG) for c in range(2)]
        sums = [seg_scan(*ends[c], jumps[c], reverse) for c in range(2)]
        for i in range(per):
            last = i * nseg if reverse else (i + 1) * nseg - 1
            for c in range(2):
                r.scb[ph, q, 4 * i + c : 4 * i + c + 1, :] = sums[c][0][last : last + 1]
                r.scb[ph, q, 4 * i + 2 + c : 4 * i + 3 + c, :] = sums[c][1][last : last + 1]
        over(1, ns, lambda k: to_seq(ph, k).start())
        first = jnp.where(place == (nseg - 1 if reverse else 0), 1.0, 0.0)
        reach = [seg_scan(first, zero, jumps[c], reverse) for c in range(2)]
        between()
        over(1, ns, lambda k: to_seq(ph, k).wait_recv())
        starts = []
        for c in range(2):
            far = power(*a[c], span)
            entering = []
            for i in range(per):
                re = jnp.zeros((1, LANES), F32)
                im = jnp.zeros((1, LANES), F32)
                for lap in range(ns):
                    j = ns - 1 - lap if reverse else lap
                    before = j > q if reverse else j < q
                    new_re, new_im = advance(
                        far,
                        (re, im),
                        (r.scb[ph, j, 4 * i + c : 4 * i + c + 1, :], r.scb[ph, j, 4 * i + 2 + c : 4 * i + 3 + c, :]),
                    )
                    re = jnp.where(before, new_re, re)
                    im = jnp.where(before, new_im, im)
                entering.append((re, im))
            in_re = jnp.broadcast_to(entering[0][0], (segs, LANES))
            in_im = jnp.broadcast_to(entering[0][1], (segs, LANES))
            for i in range(1, per):
                in_re = jnp.where(owner == i, entering[i][0], in_re)
                in_im = jnp.where(owner == i, entering[i][1], in_im)
            add_re, add_im = complex_mul(*reach[c], in_re, in_im)
            starts.append((moved(sums[c][0], 1, reverse) + add_re, moved(sums[c][1], 1, reverse) + add_im))
        return starts

    def fill_states(b, starts, a, reverse):
        for c in range(2):
            r.start[b, c] = starts[c][0]
            r.start[b, 2 + c] = starts[c][1]

        def step(i, states):
            l = SEG - 1 - i if reverse else i
            out = []
            for c in range(2):
                new = advance(a[c], states[c], (r.u[b, c, every(l), :], r.u[b, 2 + c, every(l), :]))
                r.st[b, c, every(l), :] = new[0]
                r.st[b, 2 + c, every(l), :] = new[1]
                out.append(new)
            return tuple(out)

        lax.fori_loop(0, SEG, step, tuple(starts), unroll=4)

    def fill_adjoint(b, starts, a, reverse):
        back = 1 if not reverse else -1
        zero = jnp.zeros((segs, LANES), F32)
        sums = []
        for c in range(2):
            scale_c = r.prm[b, 6:7, c * LANES : (c + 1) * LANES]

            def one(l, prior, carry, c=c, scale_c=scale_c):
                state, by_re, by_im, by_scale = carry
                re, im = advance(a[c], state, (r.adj[c, every(l), :], r.adj[2 + c, every(l), :]))
                r.adj[c, every(l), :] = scale_c * re
                r.adj[2 + c, every(l), :] = scale_c * im
                by_re = by_re + (re * prior[0] + im * prior[1])
                by_im = by_im + (im * prior[0] - re * prior[1])
                by_scale = by_scale + (re * r.u[b, c, every(l), :] + im * r.u[b, 2 + c, every(l), :])
                return (re, im), by_re, by_im, by_scale

            def step(i, carry, c=c, one=one):
                l = SEG - 1 - i if reverse else i
                prior = (r.st[b, c, every(l + back), :], r.st[b, 2 + c, every(l + back), :])
                return one(l, prior, carry)

            carry_c = lax.fori_loop(0, SEG - 1, step, (starts[c], zero, zero, zero), unroll=4)
            final = one(0 if reverse else SEG - 1, (r.start[b, c], r.start[b, 2 + c]), carry_c)
            sums.append([column_sum(x) for x in final[1:]])
        return [jnp.concatenate([sums[0][i], sums[1][i]], axis=1) for i in range(3)]

    def forward_in(b):
        gain, bias, scale_row = r.prm[b, 0:1, :], r.prm[b, 1:2, :], r.prm[b, 6:7, :]
        average = r.stat[b, 0:1, :]
        slope = r.stat[b, 1:2, :] * gain

        def tile(rows, carry):
            x = r.act[b, rows, :].astype(F32)
            scaled = (wide(r.live[rows, :]) * ((x - average) * slope + bias)).astype(BF16)
            r.scaled[b, rows, :] = scaled
            u = mm(scaled, r.win[b]) * scale_row
            for c in range(4):
                r.u[b, c, rows, :] = u[:, c * LANES : (c + 1) * LANES]
            return carry

        row_tiles(tile, 0)

    def forward_out(b, finish, init):
        skip = r.prm[b, 2:3, :]
        value_bias, gate_bias = r.prm[b, 3:4, :], r.prm[b, 4:5, :]

        def tile(rows, carry):
            readout = jnp.concatenate([r.st[b, c, rows, :] for c in range(4)], axis=1).astype(BF16)
            r.readout[b, rows, :] = readout
            mixed = mm(readout, r.wout[b]) + skip * r.scaled[b, rows, :].astype(F32)
            square = mixed * mixed
            t = jnp.tanh(ROOT * mixed * (1.0 + CUBE * square))
            half = 0.5 + 0.5 * t
            active = (mixed * half).astype(BF16)
            r.active[b, rows, :] = active
            r.slope[b, rows, :] = half + (0.5 * ROOT) * mixed * (1.0 - t * t) * (1.0 + (3.0 * CUBE) * square)
            gated = mm(active, r.wglu[b])
            gate = 0.5 + 0.5 * jnp.tanh(0.5 * (gated[:, D:] + gate_bias))
            product = (gated[:, :D] + value_bias) * gate
            live = wide(r.live[rows, :])
            result = (r.act[b, rows, :].astype(F32) + live * product).astype(BF16)
            r.act[b + 1, rows, :] = result
            return finish(rows, live, gate, product * (1.0 - gate), result, carry)

        return row_tiles(tile, init)

    def back_tile(b, rows, outer, gate, steep, carry):
        grad_gated = jnp.concatenate([outer * gate, outer * steep], axis=1).astype(BF16)
        r.gg[rows, :] = grad_gated
        grad_mixed = (r.slope[b, rows, :] * mm_t(grad_gated, r.wglu[b])).astype(BF16)
        r.gm[rows, :] = grad_mixed
        grad_readout = mm_t(grad_mixed, r.wout[b])
        for c in range(4):
            r.adj[c, rows, :] = grad_readout[:, c * LANES : (c + 1) * LANES]
        by_skip = column_sum(grad_mixed.astype(F32) * r.scaled[b, rows, :].astype(F32))
        return carry[0] + by_skip, carry[1] + column_sum(grad_gated.astype(F32))

    def normed(b, rows):
        return (r.act[b, rows, :].astype(F32) - r.stat[b, 0:1, :]) * r.stat[b, 1:2, :]

    def back_in(b):
        skip = r.prm[b, 2:3, :]

        def tile(rows, carry):
            grad_projected = jnp.concatenate([r.adj[c, rows, :] for c in range(4)], axis=1).astype(BF16)
            r.gp[rows, :] = grad_projected
            grad_scaled = skip * r.gm[rows, :].astype(F32) + mm_t(grad_projected, r.win[b])
            masked = wide(r.live[rows, :]) * grad_scaled
            r.masked[rows, :] = masked
            return carry[0] + column_sum(masked * normed(b, rows)), carry[1] + column_sum(masked)

        zero = jnp.zeros((1, D), F32)
        return row_tiles(tile, (zero, zero))

    def back_norm(ph, b):
        wait_all(ph)
        got = jnp.sum(r.bnb[ph], axis=0)
        gain_total, bias_total = as_row(got[0:4]), as_row(got[4:8])
        r.vec_tot[b, 0:1, :] = gain_total
        r.vec_tot[b, 1:2, :] = bias_total
        slope = r.stat[b, 1:2, :] * r.prm[b, 0:1, :]
        per_token = slope / r.stat[b, 2:3, :]
        return slope, per_token * bias_total, per_token * gain_total

    def source_grad(b, rows, upstream, live, slope, by_bias, by_gain):
        return upstream + live * (slope * r.masked[rows, :] - by_bias - normed(b, rows) * by_gain)

    def weight_grad(b, which, left, right):
        columns = GRAD_ROWS[which] // 4

        def tile(j, carry):
            cols = pl.ds(pl.multiple_of(j * 256, 256), 256)
            grad = t_mm(left, right[:, cols]).astype(BF16)
            at = pl.multiple_of(GRAD_AT[which] + j * 1024, 1024)
            r.dw[b, pl.ds(at, 512), :] = grad[:, :LANES]
            r.dw[b, pl.ds(at + 512, 512), :] = grad[:, LANES:]
            return carry

        lax.fori_loop(0, columns // 256, tile, 0)

    def chunk(b, which):
        rows = GRAD_ROWS[which] // 2
        return b * 3 + which, rows, GRAD_AT[which], GRAD_AT[which] // 2, rows // ns, GRAD_AT[which] // 2 // ns

    def to_core(b, which):
        n, rows, at, half_at, _, _ = chunk(b, which)
        src = r.dw.at[b, pl.ds(pl.multiple_of(at + other * rows, 16), rows)]
        return remote(src, r.sec.at[b, pl.ds(half_at, rows)], r.core_send.at[n], r.core_recv.at[n], sibling)

    def to_owner(b, which, k):
        n, _, _, half_at, piece, piece_at = chunk(b, which)
        src = r.half.at[b, pl.ds(pl.multiple_of(half_at + lax.rem(q + k, ns) * piece, 16), piece)]
        dst = r.rs.at[b, q, pl.ds(piece_at, piece)]
        return remote(src, dst, r.rs_send.at[n, k], r.rs_recv.at[n, k], seq_peer(k))

    def to_line(b, which, k):
        n, _, _, _, piece, piece_at = chunk(b, which)
        block = r.line.at[b, d, pl.ds(piece_at, piece)]
        return remote(block, block, r.line_send.at[n, k], r.line_recv.at[n, k], dp_peer(k))

    def grad_place(b, which, section, k):
        _, rows, at, _, piece, _ = chunk(b, which)
        return pl.ds(pl.multiple_of(at + section * rows + lax.rem(q + k, ns) * piece, 16), piece)

    def to_result(b, which, k):
        n, _, _, _, piece, piece_at = chunk(b, which)
        src = r.sum.at[b, pl.ds(piece_at, piece)]
        dst = r.grads.at[grad_place(b, which, s, 0)]
        target = {"section": b, "seq": lax.rem(q + k, ns)}
        return remote(src, dst, r.res_send.at[n, k], r.res_recv.at[n, s * ns + k], target)

    def from_result(b, which, section, k):
        n, _, _, _, piece, piece_at = chunk(b, which)
        src = r.sum.at[b, pl.ds(piece_at, piece)]
        dst = r.grads.at[grad_place(b, which, s, 0)]
        return remote(src, dst, r.res_send.at[n, k], r.res_recv.at[n, section * ns + k], sibling)

    def own_result(b, which):
        n, _, _, _, piece, piece_at = chunk(b, which)
        return pltpu.make_async_copy(
            r.sum.at[b, pl.ds(piece_at, piece)], r.grads.at[grad_place(b, which, s, 0)], r.own.at[n]
        )

    def step_core(b, which):
        to_core(b, which).start()

    def step_owner(b, which):
        _, rows, at, half_at, _, _ = chunk(b, which)
        to_core(b, which).wait_recv()
        mine = r.dw[b, pl.ds(pl.multiple_of(at + s * rows, 16), rows), :].astype(F32)
        r.half[b, half_at : half_at + rows, :] = (mine + r.sec[b, half_at : half_at + rows, :].astype(F32)).astype(BF16)
        over(1, ns, lambda k: to_owner(b, which, k).start())

    def step_line(b, which):
        _, _, _, half_at, piece, piece_at = chunk(b, which)
        over(1, ns, lambda k: to_owner(b, which, k).wait_recv())
        total = r.half[b, pl.ds(pl.multiple_of(half_at + q * piece, 16), piece), :].astype(F32)
        for k in range(1, ns):
            total = total + r.rs[b, lax.rem(q + k, ns), piece_at : piece_at + piece, :].astype(F32)
        r.line[b, d, piece_at : piece_at + piece, :] = total.astype(BF16)
        over(1, nd, lambda k: to_line(b, which, k).start())

    def step_result(b, which):
        _, _, _, _, piece, piece_at = chunk(b, which)
        over(1, nd, lambda k: to_line(b, which, k).wait_recv())
        total = r.line[b, 0, piece_at : piece_at + piece, :].astype(F32)
        for j in range(1, nd):
            total = total + r.line[b, j, piece_at : piece_at + piece, :].astype(F32)
        r.sum[b, piece_at : piece_at + piece, :] = total.astype(BF16)
        over(1, ns, lambda k: to_result(b, which, k).start())

        @pl.when(s == b)
        def _():
            own_result(b, which).start()

        @pl.when(s != b)
        def _():
            to_result(b, which, 0).start()

    def step_end(b, which):
        @pl.when(s == b)
        def _():
            own_result(b, which).wait()
            over(1, ns, lambda k: from_result(b, which, b, k).wait_recv())
            over(0, ns, lambda k: from_result(b, which, 1 - b, k).wait_recv())

        @pl.when(s != b)
        def _():
            to_result(b, which, 0).wait_send()

        to_core(b, which).wait_send()
        over(1, ns, lambda k: to_owner(b, which, k).wait_send())
        over(1, nd, lambda k: to_line(b, which, k).wait_send())
        over(1, ns, lambda k: to_result(b, which, k).wait_send())

    def vec_seq(b, k):
        block = r.vec_a.at[b, q]
        return remote(block, block, r.va_send.at[b, k], r.va_recv.at[b, k], seq_peer(k))

    def vec_dp(b, k):
        block = r.vec_b.at[b, d]
        return remote(block, block, r.vb_send.at[b, k], r.vb_recv.at[b, k], dp_peer(k))

    def vec_one(b, by_skip, by_bias, by_decay):
        zero = jnp.zeros((1, D), F32)
        r.vec_a[b, q, 0:1, :] = zero
        r.vec_a[b, q, 1:2, :] = zero
        r.vec_a[b, q, 2:3, :] = by_skip
        r.vec_a[b, q, 3:4, :] = by_bias[:, :D]
        r.vec_a[b, q, 4:5, :] = by_bias[:, D:]
        r.vec_a[b, q, 5:6, :] = jnp.concatenate([by_decay[0], by_decay[1]], axis=1)
        r.vec_a[b, q, 6:7, :] = jnp.concatenate([by_decay[2], by_decay[2]], axis=1)
        r.vec_a[b, q, 7:8, :] = zero
        over(1, ns, lambda k: vec_seq(b, k).start())

    def vec_two(b):
        over(1, ns, lambda k: vec_seq(b, k).wait_recv())
        r.vec_b[b, d] = jnp.sum(r.vec_a[b], axis=0)
        over(1, nd, lambda k: vec_dp(b, k).start())

    def vec_three(b):
        over(1, nd, lambda k: vec_dp(b, k).wait_recv())
        total = jnp.sum(r.vec_b[b], axis=0)
        r.vec_tot[b, 2:8, :] = total[2:8]

    send_prm.wait_recv()
    for i in range(3):
        load_w[i].wait()
        send_w[i].wait_recv()
    load_cot.wait()
    zero_row = jnp.zeros((1, D), F32)

    def nothing():
        pass

    norm_merge(0)
    forward_in(0)
    ahead0, ahead1 = decay(0, 1.0), decay(1, 1.0)
    starts = carry(0, r.u.at[0], ahead0, False, nothing)
    fill_states(0, starts, ahead0, False)

    def finish_one(rows, live, gate, steep, result, carry):
        r.gate[rows, :] = gate
        r.steep[rows, :] = steep
        return carry + column_sum(result.astype(F32))

    norm_sums(1, forward_out(0, finish_one, zero_row))
    send_all(1)
    norm_merge(1)
    forward_in(1)
    starts = carry(1, r.u.at[1], ahead1, True, nothing)
    fill_states(1, starts, ahead1, True)

    def finish_two(rows, live, gate, steep, result, carry):
        return back_tile(1, rows, live * r.cotv[rows, :].astype(F32), gate, steep, carry)

    wide_zero = jnp.zeros((1, 2 * D), F32)
    by_skip, by_bias = forward_out(1, finish_two, (zero_row, wide_zero))

    keep_act = pltpu.make_async_copy(r.act.at[1 + s], r.act_out.at[s], r.local.at[5])
    keep_act.start()
    give_act = remote(r.act.at[1 + other], r.act_out.at[s], r.far_send.at[4], r.far_recv.at[4], sibling)
    give_act.start()

    back0, back1 = decay(0, -1.0), decay(1, -1.0)

    def glu_and_out(b):
        weight_grad(b, GLU, r.active[b], r.gg)
        step_core(b, GLU)
        weight_grad(b, OUT, r.readout[b], r.gm)
        step_core(b, OUT)

    starts = carry(2, r.adj, back1, False, lambda: glu_and_out(1))
    by_decay = fill_adjoint(1, starts, back1, False)
    put_rows(2, *back_in(1))
    send_all(2)
    step_owner(1, GLU)
    step_owner(1, OUT)
    vec_one(1, by_skip, by_bias, by_decay)
    weight_grad(1, IN, r.scaled[1], r.gp)
    step_core(1, IN)
    slope, by_bias_total, by_gain_total = back_norm(2, 1)

    def through(rows, carry):
        live = wide(r.live[rows, :])
        upstream = r.cotv[rows, :].astype(F32)
        grad = source_grad(1, rows, upstream, live, slope, by_bias_total, by_gain_total).astype(BF16)
        r.ig[1, rows, :] = grad
        return back_tile(0, rows, live * grad.astype(F32), r.gate[rows, :], r.steep[rows, :], carry)

    by_skip, by_bias = row_tiles(through, (zero_row, wide_zero))

    def next_pieces():
        step_line(1, GLU)
        step_line(1, OUT)
        step_owner(1, IN)
        vec_two(1)
        glu_and_out(0)

    starts = carry(3, r.adj, back0, True, next_pieces)
    by_decay = fill_adjoint(0, starts, back0, True)
    put_rows(3, *back_in(0))
    send_all(3)
    weight_grad(0, IN, r.scaled[0], r.gp)
    step_core(0, IN)
    step_owner(0, GLU)
    step_owner(0, OUT)
    vec_one(0, by_skip, by_bias, by_decay)
    step_line(1, IN)
    step_result(1, GLU)
    step_result(1, OUT)
    vec_three(1)
    slope0, by_bias_total0, by_gain_total0 = back_norm(3, 0)

    def last(rows, carry):
        live = wide(r.live[rows, :])
        upstream = r.ig[1, rows, :].astype(F32)
        grad = source_grad(0, rows, upstream, live, slope0, by_bias_total0, by_gain_total0)
        r.ig[0, rows, :] = (live * grad).astype(BF16)
        return carry

    row_tiles(last, 0)
    keep_ig = pltpu.make_async_copy(r.ig.at[s], r.ig_out.at[s], r.local.at[6])
    keep_ig.start()
    give_ig = remote(r.ig.at[other], r.ig_out.at[s], r.far_send.at[5], r.far_recv.at[5], sibling)
    give_ig.start()

    step_owner(0, IN)
    step_line(0, GLU)
    step_line(0, OUT)
    step_result(1, IN)
    vec_two(0)
    step_line(0, IN)
    step_result(0, GLU)
    step_result(0, OUT)
    vec_three(0)
    give_vec = remote(r.vec_tot.at[other], r.vec_far, r.far_send.at[6], r.far_recv.at[6], sibling)
    give_vec.start()
    step_result(0, IN)
    give_vec.wait_recv()
    total = r.vec_tot[s] + r.vec_far[...]
    r.o_gain[...] = total[0:1]
    r.o_bias[...] = total[1:2]
    r.o_skip[...] = total[2:3]
    r.o_bglu[:, :D] = total[3:4]
    r.o_bglu[:, D:] = total[4:5]
    grad_re, grad_im = total[5:6, :STATES], total[5:6, STATES:]
    grad_rate = total[6:7, :STATES] * jnp.exp(-double) / scale_sq - (grad_re * decay_re + grad_im * decay_im)
    r.o_nu[...] = grad_rate * rate
    r.o_theta[...] = (grad_im * decay_re - grad_re * decay_im) * phase

    for b in (1, 0):
        for which in (GLU, OUT, IN):
            step_end(b, which)
    keep_act.wait()
    give_act.wait()
    keep_ig.wait()
    give_ig.wait()
    give_vec.wait_send()
    send_prm.wait_send()
    for copy in send_w:
        copy.wait_send()
    for ph in range(4):
        over(1, peers, lambda k, ph=ph: to_all(ph, k).wait_send())
        over(1, ns, lambda k, ph=ph: to_seq(ph, k).wait_send())
    for b in range(2):
        over(1, ns, lambda k, b=b: vec_seq(b, k).wait_send())
        over(1, nd, lambda k, b=b: vec_dp(b, k).wait_send())


def body(ns, nd, inputs, mask, gain, bias, nu, theta, w_in, w_out, skip, w_glu, b_glu, cotangent):
    per = inputs.shape[0] // MICRO
    span = inputs.shape[1]
    tokens = per * span
    segs = tokens // SEG
    dma = pltpu.SemaphoreType.DMA
    vmem = pltpu.VMEM
    names_in = ["x", "cot", "mask", "gain", "bias", "nu", "theta", "skip", "bglu", "w_in", "w_out", "w_glu"]
    any_in = {"x", "cot", "w_in", "w_out", "w_glu"}
    outs = {
        "act_out": jax.ShapeDtypeStruct((MICRO, tokens, D), BF16),
        "ig_out": jax.ShapeDtypeStruct((MICRO, tokens, D), BF16),
        "grads": jax.ShapeDtypeStruct((ALL_ROWS, LANES), BF16),
        "o_gain": jax.ShapeDtypeStruct((1, D), F32),
        "o_bias": jax.ShapeDtypeStruct((1, D), F32),
        "o_nu": jax.ShapeDtypeStruct((1, STATES), F32),
        "o_theta": jax.ShapeDtypeStruct((1, STATES), F32),
        "o_skip": jax.ShapeDtypeStruct((1, D), F32),
        "o_bglu": jax.ShapeDtypeStruct((1, 2 * D), F32),
    }
    any_out = {"act_out", "ig_out", "grads"}
    half = ALL_ROWS // 2
    scratch = {
        "act": vmem((3, tokens, D), BF16),
        "cotv": vmem((tokens, D), BF16),
        "live": vmem((tokens, LANES), F32),
        "win": vmem((2, D, D), BF16),
        "wout": vmem((2, D, D), BF16),
        "wglu": vmem((2, D, 2 * D), BF16),
        "prm": vmem((2, 8, D), F32),
        "stat": vmem((2, 8, D), F32),
        "scaled": vmem((2, tokens, D), BF16),
        "u": vmem((2, 4, tokens, LANES), F32),
        "st": vmem((2, 4, tokens, LANES), F32),
        "start": vmem((2, 4, segs, LANES), F32),
        "readout": vmem((2, tokens, D), BF16),
        "active": vmem((2, tokens, D), BF16),
        "slope": vmem((2, tokens, D), F32),
        "gate": vmem((tokens, D), F32),
        "steep": vmem((tokens, D), F32),
        "gg": vmem((tokens, 2 * D), BF16),
        "gm": vmem((tokens, D), BF16),
        "adj": vmem((4, tokens, LANES), F32),
        "gp": vmem((tokens, D), BF16),
        "masked": vmem((tokens, D), F32),
        "ig": vmem((2, tokens, D), BF16),
        "bnb": vmem((4, ns * nd, 9, LANES), F32),
        "scb": vmem((4, ns, 4 * per, LANES), F32),
        "dw": vmem((2, ALL_ROWS, LANES), BF16),
        "sec": vmem((2, half, LANES), BF16),
        "half": vmem((2, half, LANES), BF16),
        "rs": vmem((2, ns, half // ns, LANES), BF16),
        "line": vmem((2, nd, half // ns, LANES), BF16),
        "sum": vmem((2, half // ns, LANES), BF16),
        "vec_a": vmem((2, ns, 8, D), F32),
        "vec_b": vmem((2, nd, 8, D), F32),
        "vec_tot": vmem((2, 8, D), F32),
        "vec_far": vmem((8, D), F32),
        "local": dma((7,)),
        "own": dma((6,)),
        "far_send": dma((7,)),
        "far_recv": dma((7,)),
        "bn_send": dma((4, ns * nd)),
        "bn_recv": dma((4, ns * nd)),
        "sc_send": dma((4, ns)),
        "sc_recv": dma((4, ns)),
        "core_send": dma((6,)),
        "core_recv": dma((6,)),
        "rs_send": dma((6, ns)),
        "rs_recv": dma((6, ns)),
        "line_send": dma((6, nd)),
        "line_recv": dma((6, nd)),
        "res_send": dma((6, ns)),
        "res_recv": dma((6, 2 * ns)),
        "va_send": dma((2, ns)),
        "va_recv": dma((2, ns)),
        "vb_send": dma((2, nd)),
        "vb_recv": dma((2, nd)),
    }
    in_any = pl.BlockSpec(memory_space=pl.ANY)
    in_vmem = pl.BlockSpec(memory_space=pltpu.VMEM)
    names = names_in + list(outs) + list(scratch)
    act, ig, grads, d_gain, d_bias, d_nu, d_theta, d_skip, d_bglu = pl.pallas_call(
        functools.partial(kernel, ns, nd, per, span, names),
        out_shape=list(outs.values()),
        in_specs=[in_any if name in any_in else in_vmem for name in names_in],
        out_specs=[in_any if name in any_out else in_vmem for name in outs],
        scratch_shapes=list(scratch.values()),
        compiler_params=pltpu.CompilerParams(
            collective_id=0, has_side_effects=True, vmem_limit_bytes=60 * 2**20
        ),
    )(
        inputs.reshape(MICRO, tokens, D),
        cotangent.reshape(MICRO, tokens, D),
        mask,
        gain,
        bias,
        nu,
        theta,
        skip,
        b_glu,
        w_in,
        w_out,
        w_glu,
    )

    def matrix(which):
        part = grads[GRAD_AT[which] : GRAD_AT[which] + GRAD_ROWS[which]].reshape(-1, D, LANES)
        return jnp.transpose(part, (1, 0, 2)).reshape(1, D, -1).astype(F32)

    whole = (1, MICRO * per, span, D)
    return (
        act.reshape(whole),
        ig.reshape(whole).astype(F32),
        d_gain,
        d_bias,
        d_nu,
        d_theta,
        matrix(IN),
        matrix(OUT),
        d_skip,
        matrix(GLU),
        d_bglu,
    )


def solution(mesh):
    rows = P("section", None)
    cube = P("section", None, None)
    tokens = P("dp", "seq", None)
    spread = P("section", "dp", "seq", None)
    in_specs = (tokens, P("dp", "seq"), rows, rows, rows, rows, cube, cube, rows, cube, rows, tokens)
    out_specs = (spread, spread, rows, rows, rows, rows, cube, cube, rows, cube, rows)
    return jax.shard_map(
        functools.partial(body, mesh.shape["seq"], mesh.shape["dp"]),
        mesh=mesh,
        in_specs=in_specs,
        out_specs=out_specs,
        check_vma=False,
    )
```

profile of v0, /device:TPU:0, one launch (start us, length us, event | category | flops | bytes accessed | tf_op | source)
XLA Modules:
  0.0 145.5 jit_solution(8479514099941350888)
XLA Ops:
  0.6 126.5 %shard_map.203 = (bf16[2,1024,512]{2,1,0:T(8,128)(2,1)}, bf16[2,1024,512]{2,1,0:T(8,128)(2,1)}, bf16[8192,128]{1,0:T(8,128)(2,1)}, f32[1,512]{1,0:T(1,128)}, f32...) custom-call(bf16[2,1024,512]{2,1,0:T(8,128)(2,1)} %refs_0_.1, ...), custom_call_target="tpu_custom_call" | custom-call | tf_op jit(solution)/shard_map/pallas_call | solution.py:790
  127.2 0.0 copy-start.1
  127.2 1.4 slice.11
  128.6 0.5 copy-done.1
  129.1 0.1 fusion
  129.2 0.1 convert_bitcast_fusion.2
  129.2 0.7 copy.23
  129.9 1.4 reshape.84
  131.3 0.1 convert_bitcast_fusion.1
  131.4 0.7 copy.24
  132.1 1.4 reshape.85
  133.5 0.1 convert_bitcast_fusion
  133.6 1.2 copy.25
  134.8 1.5 %reshape.86 = f32[1,512,1024]{2,1,0:T(8,128)} reshape(f32[512,8,128]{2,1,0:T(8,128)S(1)} %copy.25) | data formatting | bytes 4194304 | tf_op jit(solution)/shard_map/convert_element_type | solution.py:816
  136.3 0.0 copy-start
  136.3 4.3 %bitcast_convert_fusion = f32[1,2,1024,512]{3,2,1,0:T(8,128)} fusion(bf16[2,1024,512]{2,1,0:T(8,128)(2,1)} %get-tuple-element.21), kind=kLoop, calls=%fused_computation.1 | loop fusion | flops 1048576 | bytes 6291456 | tf_op jit(solution)/shard_map/convert_element_type | solution.py:821
  140.7 0.0 copy-done
  140.7 0.0 copy-start.5
  140.7 0.0 copy-start.4
  140.7 0.0 copy-start.7
  140.7 0.0 copy-start.6
  140.7 0.0 copy-start.3
  140.7 0.0 copy-start.2
  140.7 1.3 copy.33
  142.0 0.0 copy-done.5
  142.0 0.6 copy.34
  142.6 0.0 copy-done.4
  142.6 0.6 copy.35
  143.2 0.0 copy-done.7
  143.2 0.6 copy.36
  143.8 0.0 copy-done.6
  143.8 0.6 copy.37
  144.3 0.0 copy-done.3
  144.3 0.6 copy.38
  144.9 0.0 copy-done.2
  144.9 0.6 copy.39
Async XLA Ops:
  127.2 1.9 %copy-start.1 = (bf16[8192,128]{1,0:T(8,128)(2,1)S(1)}, bf16[8192,128]{1,0:T(8,128)(2,1)}, u32[]{:S(2)}) copy-start(bf16[8192,128]{1,0:T(8,128)(2,1)} %get-tuple-element.26) | copy-start | bytes 6291460
  136.3 4.4 %copy-start = (bf16[2,1024,512]{2,1,0:T(8,128)(2,1)S(1)}, bf16[2,1024,512]{2,1,0:T(8,128)(2,1)}, u32[]{:S(2)}) copy-start(bf16[2,1024,512]{2,1,0:T(8,128)(2,1)} %get-tuple-element.20) | copy-start | bytes 6291460
  140.7 1.4 copy-start.5
  140.7 1.9 %copy-start.4 = (f32[1,512]{1,0:T(1,128)S(1)}, f32[1,512]{1,0:T(1,128)}, u32[]{:S(2)}) copy-start(f32[1,512]{1,0:T(1,128)} %get-tuple-element.45) | copy-start | bytes 6148
  140.7 2.5 %copy-start.7 = (f32[1,256]{1,0:T(1,128)S(1)}, f32[1,256]{1,0:T(1,128)}, u32[]{:S(2)}) copy-start(f32[1,256]{1,0:T(1,128)} %get-tuple-element.46) | copy-start | bytes 3076
  140.7 3.1 %copy-start.6 = (f32[1,256]{1,0:T(1,128)S(1)}, f32[1,256]{1,0:T(1,128)}, u32[]{:S(2)}) copy-start(f32[1,256]{1,0:T(1,128)} %get-tuple-element.47) | copy-start | bytes 3076
  140.7 3.6 %copy-start.3 = (f32[1,512]{1,0:T(1,128)S(1)}, f32[1,512]{1,0:T(1,128)}, u32[]{:S(2)}) copy-start(f32[1,512]{1,0:T(1,128)} %get-tuple-element.50) | copy-start | bytes 6148
  140.7 4.2 %copy-start.2 = (f32[1,1024]{1,0:T(1,128)S(1)}, f32[1,1024]{1,0:T(1,128)}, u32[]{:S(2)}) copy-start(f32[1,1024]{1,0:T(1,128)} %get-tuple-element.52) | copy-start | bytes 12292
where the time goes:
time: 146 us; the launch traced here: 145 us
  Pallas kernels  127 us (87%)
  local copies, waits for them, and re-layouts  13.6 us (9%)
  other arithmetic  4.62 us (3%)
    pallas_call x1, Pallas kernels, body(): pl.pallas_call(functools.partial(kernel, ns, nd, per, span, names), out_s...  127 us
    convert_element_type x6, local copies, waits for them, and re-layouts, matrix(): return jnp.transpose(part, (1, 0, 2)).reshape(1, D, -1).astype(F32)  6.84 us
    unnamed x23, local copies, waits for them, and re-layouts  5.25 us
    convert_element_type x1, other arithmetic, body(): ig.reshape(whole).astype(F32)  4.35 us

commit v1 on v0

--- a/solution.py
+++ b/solution.py
@@ -16,10 +16,23 @@
 LANES = 128
 ROWS = 256
 SEG = 32
+EIGHT = 8
 GLU, OUT, IN = 0, 1, 2
 GRAD_ROWS = (4096, 2048, 2048)
 GRAD_AT = (0, 4096, 6144)
 ALL_ROWS = 8192
+ORDERS = (("seq", "dp"), ("seq", "dp"), ("seq", "dp"), ("seq", "dp"), ("seq", "dp"), ("seq", "dp"))
+PLAN = (
+    "in1",
+    "glu1 out1",
+    "in1",
+    "glu0 out0",
+    "in0 glu1 out1 in1",
+    "",
+    "glu1 out1 in1 glu0 out0",
+    "in0 glu0 out0",
+    "in0 glu0 out0 in0",
+)
 ROOT = math.sqrt(2.0 / math.pi)
 CUBE = 0.044715
 
@@ -67,12 +80,36 @@
     return jnp.sum(x, axis=0, keepdims=True)
 
 
+def slots_of(rows, counts, spread):
+    out, start = [], 0
+    for level, count in enumerate(counts):
+        size = rows if spread and level == len(counts) - 1 else rows // count
+        out.append((start, size))
+        start += count * size
+        rows //= count
+    return out
+
+
+def slot_rows(ns, nd):
+    inner = next(n for n in range(math.isqrt(ns), 0, -1) if ns % n == 0)
+    sizes = {"seq": ns, "dp": nd, "in": inner, "out": ns // inner}
+    bases = [0]
+    for n, order in enumerate(ORDERS):
+        rows = GRAD_ROWS[n % 3] // 2
+        counts = [sizes[name] for name in order]
+        spread = rows // math.prod(counts) % 16 != 0
+        start, size = slots_of(rows, counts, spread)[-1]
+        bases.append(bases[-1] + start + counts[-1] * size)
+    return bases
+
+
 def kernel(ns, nd, per, span, names, *refs):
     r = types.SimpleNamespace(**dict(zip(names, refs)))
     tokens = per * span
     segs = tokens // SEG
     nseg = span // SEG
     tiles = tokens // ROWS
+    blocks = segs // EIGHT
     peers = ns * nd
     s = lax.axis_index("section")
     d = lax.axis_index("dp")
@@ -105,6 +142,8 @@
 
         return lax.fori_loop(0, tiles, step, init)
 
+    slot_base = slot_rows(ns, nd)
+
     barrier = pltpu.get_barrier_semaphore()
 
     def greet(device):
@@ -112,7 +151,8 @@
 
     greet(sibling)
     over(1, peers, lambda k: greet(any_peer(k)))
-    over(1, ns, lambda k: greet({"section": other, "seq": lax.rem(q + k, ns)}))
+    over(1, ns, lambda k: greet({"section": other, **seq_peer(k)}))
+    over(1, nd, lambda k: greet({"section": other, **dp_peer(k)}))
 
     load_x = pltpu.make_async_copy(r.x.at[s], r.act.at[0], r.local.at[0])
     load_x.start()
@@ -146,16 +186,25 @@
     r.prm[s, 7:8, :] = jnp.zeros((1, D), F32)
 
     count = jnp.zeros((1, 1), F32)
-    steps = lax.broadcasted_iota(jnp.int32, (span, LANES), 0)
+    row = lax.broadcasted_iota(jnp.int32, (tokens, LANES), 0)
+    inside = lax.rem(row, ROWS)
+    token = row - inside + lax.rem(inside, EIGHT) * SEG + inside // EIGHT
+    step_of = lax.rem(token, span)
+    sequence = token // span
+    ends_at = jnp.zeros((tokens, LANES), jnp.int32)
     for i in range(per):
         here = jnp.sum(r.mask[pl.ds(s * per + i, 1), :], axis=1, keepdims=True)
-        r.live[i * span : (i + 1) * span, :] = jnp.where(steps < here, 1.0, 0.0)
+        ends_at = jnp.where(sequence == i, here, ends_at)
         count = count + here.astype(F32)
+    r.live[...] = jnp.where(step_of < ends_at, 1.0, 0.0)
     count_row = jnp.broadcast_to(count, (1, LANES))
+    to_row = lax.broadcasted_iota(jnp.int32, (ROWS, ROWS), 0)
+    from_row = lax.broadcasted_iota(jnp.int32, (ROWS, ROWS), 1)
+    r.order[...] = jnp.where(from_row == lax.rem(to_row, EIGHT) * SEG + to_row // EIGHT, 1.0, 0.0).astype(BF16)
     load_x.wait()
 
     def mask_input(rows, total):
-        x = r.act[0, rows, :].astype(F32) * wide(r.live[rows, :])
+        x = mm(r.order[...], r.act[0, rows, :]) * wide(r.live[rows, :])
         r.act[0, rows, :] = x.astype(BF16)
         return total + column_sum(x)
 
@@ -200,7 +249,7 @@
 
     norm_sums(0, row_tiles(mask_input, jnp.zeros((1, D), F32)))
 
-    pl.semaphore_wait(barrier, peers + ns - 1)
+    pl.semaphore_wait(barrier, peers + ns - 1 + nd - 1)
     send_all(0)
     send_prm = remote(r.prm.at[s], r.prm.at[s], r.far_send.at[0], r.far_recv.at[0], sibling)
     send_prm.start()
@@ -219,8 +268,15 @@
             out.append((re, sign * im))
         return out
 
-    def every(l):
-        return pl.ds(l, segs, stride=SEG)
+    def step_rows(k, l):
+        return pl.ds(pl.multiple_of(k * ROWS + l * EIGHT, EIGHT), EIGHT)
+
+    def at_step(ref, l):
+        return jnp.concatenate([ref[step_rows(k, l), :] for k in range(blocks)], axis=0)
+
+    def put_step(ref, l, value):
+        for k in range(blocks):
+            ref[step_rows(k, l), :] = value[k * EIGHT : (k + 1) * EIGHT]
 
     def advance(a, state, drive):
         return (
@@ -253,7 +309,7 @@
         def step(i, states):
             l = SEG - 1 - i if reverse else i
             return tuple(
-                advance(a[c], states[c], (drive[c, every(l), :], drive[2 + c, every(l), :])) for c in range(2)
+                advance(a[c], states[c], (at_step(drive.at[c], l), at_step(drive.at[2 + c], l))) for c in range(2)
             )
 
         zero = jnp.zeros((segs, LANES), F32)
@@ -306,9 +362,9 @@
             l = SEG - 1 - i if reverse else i
             out = []
             for c in range(2):
-                new = advance(a[c], states[c], (r.u[b, c, every(l), :], r.u[b, 2 + c, every(l), :]))
-                r.st[b, c, every(l), :] = new[0]
-                r.st[b, 2 + c, every(l), :] = new[1]
+                new = advance(a[c], states[c], (at_step(r.u.at[b, c], l), at_step(r.u.at[b, 2 + c], l)))
+                put_step(r.st.at[b, c], l, new[0])
+                put_step(r.st.at[b, 2 + c], l, new[1])
                 out.append(new)
             return tuple(out)
 
@@ -323,17 +379,17 @@
 
             def one(l, prior, carry, c=c, scale_c=scale_c):
                 state, by_re, by_im, by_scale = carry
-                re, im = advance(a[c], state, (r.adj[c, every(l), :], r.adj[2 + c, every(l), :]))
-                r.adj[c, every(l), :] = scale_c * re
-                r.adj[2 + c, every(l), :] = scale_c * im
+                re, im = advance(a[c], state, (at_step(r.adj.at[c], l), at_step(r.adj.at[2 + c], l)))
+                put_step(r.adj.at[c], l, scale_c * re)
+                put_step(r.adj.at[2 + c], l, scale_c * im)
                 by_re = by_re + (re * prior[0] + im * prior[1])
                 by_im = by_im + (im * prior[0] - re * prior[1])
-                by_scale = by_scale + (re * r.u[b, c, every(l), :] + im * r.u[b, 2 + c, every(l), :])
+                by_scale = by_scale + (re * at_step(r.u.at[b, c], l) + im * at_step(r.u.at[b, 2 + c], l))
                 return (re, im), by_re, by_im, by_scale
 
             def step(i, carry, c=c, one=one):
                 l = SEG - 1 - i if reverse else i
-                prior = (r.st[b, c, every(l + back), :], r.st[b, 2 + c, every(l + back), :])
+                prior = (at_step(r.st.at[b, c], l + back), at_step(r.st.at[b, 2 + c], l + back))
                 return one(l, prior, carry)
 
             carry_c = lax.fori_loop(0, SEG - 1, step, (starts[c], zero, zero, zero), unroll=4)
@@ -400,10 +456,10 @@
 
         def tile(rows, carry):
             grad_projected = jnp.concatenate([r.adj[c, rows, :] for c in range(4)], axis=1).astype(BF16)
-            r.gp[rows, :] = grad_projected
+            r.readout[b, rows, :] = grad_projected
             grad_scaled = skip * r.gm[rows, :].astype(F32) + mm_t(grad_projected, r.win[b])
             masked = wide(r.live[rows, :]) * grad_scaled
-            r.masked[rows, :] = masked
+            r.slope[b, rows, :] = masked
             return carry[0] + column_sum(masked * normed(b, rows)), carry[1] + column_sum(masked)
 
         zero = jnp.zeros((1, D), F32)
@@ -420,7 +476,7 @@
         return slope, per_token * bias_total, per_token * gain_total
 
     def source_grad(b, rows, upstream, live, slope, by_bias, by_gain):
-        return upstream + live * (slope * r.masked[rows, :] - by_bias - normed(b, rows) * by_gain)
+        return upstream + live * (slope * r.slope[b, rows, :] - by_bias - normed(b, rows) * by_gain)
 
     def weight_grad(b, which, left, right):
         columns = GRAD_ROWS[which] // 4
@@ -435,100 +491,157 @@
 
         lax.fori_loop(0, columns // 256, tile, 0)
 
-    def chunk(b, which):
-        rows = GRAD_ROWS[which] // 2
-        return b * 3 + which, rows, GRAD_AT[which], GRAD_AT[which] // 2, rows // ns, GRAD_AT[which] // 2 // ns
-
-    def to_core(b, which):
-        n, rows, at, half_at, _, _ = chunk(b, which)
-        src = r.dw.at[b, pl.ds(pl.multiple_of(at + other * rows, 16), rows)]
-        return remote(src, r.sec.at[b, pl.ds(half_at, rows)], r.core_send.at[n], r.core_recv.at[n], sibling)
-
-    def to_owner(b, which, k):
-        n, _, _, half_at, piece, piece_at = chunk(b, which)
-        src = r.half.at[b, pl.ds(pl.multiple_of(half_at + lax.rem(q + k, ns) * piece, 16), piece)]
-        dst = r.rs.at[b, q, pl.ds(piece_at, piece)]
-        return remote(src, dst, r.rs_send.at[n, k], r.rs_recv.at[n, k], seq_peer(k))
-
-    def to_line(b, which, k):
-        n, _, _, _, piece, piece_at = chunk(b, which)
-        block = r.line.at[b, d, pl.ds(piece_at, piece)]
-        return remote(block, block, r.line_send.at[n, k], r.line_recv.at[n, k], dp_peer(k))
-
-    def grad_place(b, which, section, k):
-        _, rows, at, _, piece, _ = chunk(b, which)
-        return pl.ds(pl.multiple_of(at + section * rows + lax.rem(q + k, ns) * piece, 16), piece)
-
-    def to_result(b, which, k):
-        n, _, _, _, piece, piece_at = chunk(b, which)
-        src = r.sum.at[b, pl.ds(piece_at, piece)]
-        dst = r.grads.at[grad_place(b, which, s, 0)]
-        target = {"section": b, "seq": lax.rem(q + k, ns)}
-        return remote(src, dst, r.res_send.at[n, k], r.res_recv.at[n, s * ns + k], target)
-
-    def from_result(b, which, section, k):
-        n, _, _, _, piece, piece_at = chunk(b, which)
-        src = r.sum.at[b, pl.ds(piece_at, piece)]
-        dst = r.grads.at[grad_place(b, which, s, 0)]
-        return remote(src, dst, r.res_send.at[n, k], r.res_recv.at[n, section * ns + k], sibling)
-
-    def own_result(b, which):
-        n, _, _, _, piece, piece_at = chunk(b, which)
-        return pltpu.make_async_copy(
-            r.sum.at[b, pl.ds(piece_at, piece)], r.grads.at[grad_place(b, which, s, 0)], r.own.at[n]
-        )
-
-    def step_core(b, which):
-        to_core(b, which).start()
-
-    def step_owner(b, which):
-        _, rows, at, half_at, _, _ = chunk(b, which)
-        to_core(b, which).wait_recv()
-        mine = r.dw[b, pl.ds(pl.multiple_of(at + s * rows, 16), rows), :].astype(F32)
-        r.half[b, half_at : half_at + rows, :] = (mine + r.sec[b, half_at : half_at + rows, :].astype(F32)).astype(BF16)
-        over(1, ns, lambda k: to_owner(b, which, k).start())
-
-    def step_line(b, which):
-        _, _, _, half_at, piece, piece_at = chunk(b, which)
-        over(1, ns, lambda k: to_owner(b, which, k).wait_recv())
-        total = r.half[b, pl.ds(pl.multiple_of(half_at + q * piece, 16), piece), :].astype(F32)
-        for k in range(1, ns):
-            total = total + r.rs[b, lax.rem(q + k, ns), piece_at : piece_at + piece, :].astype(F32)
-        r.line[b, d, piece_at : piece_at + piece, :] = total.astype(BF16)
-        over(1, nd, lambda k: to_line(b, which, k).start())
-
-    def step_result(b, which):
-        _, _, _, _, piece, piece_at = chunk(b, which)
-        over(1, nd, lambda k: to_line(b, which, k).wait_recv())
-        total = r.line[b, 0, piece_at : piece_at + piece, :].astype(F32)
-        for j in range(1, nd):
-            total = total + r.line[b, j, piece_at : piece_at + piece, :].astype(F32)
-        r.sum[b, piece_at : piece_at + piece, :] = total.astype(BF16)
-        over(1, ns, lambda k: to_result(b, which, k).start())
-
-        @pl.when(s == b)
-        def _():
-            own_result(b, which).start()
-
-        @pl.when(s != b)
-        def _():
-            to_result(b, which, 0).start()
-
-    def step_end(b, which):
-        @pl.when(s == b)
-        def _():
-            own_result(b, which).wait()
-            over(1, ns, lambda k: from_result(b, which, b, k).wait_recv())
-            over(0, ns, lambda k: from_result(b, which, 1 - b, k).wait_recv())
-
-        @pl.when(s != b)
-        def _():
-            to_result(b, which, 0).wait_send()
-
-        to_core(b, which).wait_send()
-        over(1, ns, lambda k: to_owner(b, which, k).wait_send())
-        over(1, nd, lambda k: to_line(b, which, k).wait_send())
-        over(1, ns, lambda k: to_result(b, which, k).wait_send())
+    inner = next(n for n in range(math.isqrt(ns), 0, -1) if ns % n == 0)
+    outer = ns // inner
+    q_out, q_in = q // inner, lax.rem(q, inner)
+    axes = {
+        "seq": (ns, q, seq_peer),
+        "dp": (nd, d, dp_peer),
+        "in": (inner, q_in, lambda k: {"seq": q_out * inner + lax.rem(q_in + k, inner)}),
+        "out": (outer, q_out, lambda k: {"seq": lax.rem(q_out + k, outer) * inner + q_in}),
+    }
+
+    class Reduced:
+        def __init__(self, b, which):
+            self.b, self.n, self.at = b, b * 3 + which, GRAD_AT[which]
+            self.base = self.at // 2
+            self.axes = [axes[name] for name in ORDERS[self.n]]
+            self.sizes, self.offsets = [GRAD_ROWS[which] // 2], [0]
+            for count, index, _ in self.axes:
+                self.sizes.append(self.sizes[-1] // count)
+                self.offsets.append(self.offsets[-1] + index * self.sizes[-1])
+            self.spread = self.sizes[-1] % 16 != 0
+            self.slots = slots_of(GRAD_ROWS[which] // 2, [count for count, _, _ in self.axes], self.spread)
+            self.slot_base = slot_base[self.n]
+            self.steps = self.plan()
+
+        def rows(self, offset, size):
+            return pl.ds(pl.multiple_of(self.base + offset, 16), size)
+
+        def to_core(self):
+            size = self.sizes[0]
+            src = r.dw.at[self.b, pl.ds(pl.multiple_of(self.at + other * size, 16), size)]
+            return remote(src, r.sec.at[self.b, self.rows(0, size)], r.core_send.at[self.n], r.core_recv.at[self.n], sibling)
+
+        def slot(self, level, index):
+            start, size = self.slots[level]
+            return pl.ds(pl.multiple_of(self.slot_base + start + index * size, 16), size)
+
+        def scatter(self, level, k):
+            count, index, peer = self.axes[level]
+            if self.spread and level == len(self.axes) - 1:
+                src = r.slots.at[self.slot(level, index)]
+            else:
+                size = self.sizes[level + 1]
+                src = r.half.at[self.b, self.rows(self.offsets[level] + lax.rem(index + k, count) * size, size)]
+            dst = r.slots.at[self.slot(level, index)]
+            return remote(src, dst, r.rs_send.at[self.n, level, k], r.rs_recv.at[self.n, level, k], peer(k))
+
+        def gather(self, level, k):
+            block = r.gat.at[self.b, self.rows(self.offsets[level + 1], self.sizes[level + 1])]
+            return remote(
+                block, block, r.ag_send.at[self.n, level, k], r.ag_recv.at[self.n, level, k], self.axes[level][2](k)
+            )
+
+        def place(self):
+            return pl.ds(pl.multiple_of(self.at + s * self.sizes[0] + self.offsets[1], 16), self.sizes[1])
+
+        def result(self, k, section):
+            src = r.gat.at[self.b, self.rows(self.offsets[1], self.sizes[1])]
+            recv = r.ag_recv.at[self.n, 0, section * self.axes[0][0] + k]
+            target = {"section": self.b, **self.axes[0][2](k)} if not isinstance(k, int) or k else {"section": self.b}
+            return remote(src, r.grads.at[self.place()], r.ag_send.at[self.n, 0, k], recv, target)
+
+        def own(self):
+            src = r.gat.at[self.b, self.rows(self.offsets[1], self.sizes[1])]
+            return pltpu.make_async_copy(src, r.grads.at[self.place()], r.own.at[self.n])
+
+        def each(self, level, body):
+            over(1, self.axes[level][0], body)
+
+        def first(self):
+            size = self.sizes[0]
+            self.to_core().wait_recv()
+            mine = r.dw[self.b, pl.ds(pl.multiple_of(self.at + s * size, 16), size), :].astype(F32)
+            there = r.sec[self.b, self.base : self.base + size, :].astype(F32)
+            r.half[self.b, self.base : self.base + size, :] = (mine + there).astype(BF16)
+
+        def collect(self, level):
+            self.each(level, lambda k: self.scatter(level, k).wait_recv())
+            count, index, _ = self.axes[level]
+            last = level == len(self.axes) - 1
+            if self.spread and last:
+                total = sum(r.slots[self.slot(level, j), :].astype(F32) for j in range(count))
+                r.gat[self.b, self.rows(self.offsets[level], self.sizes[level]), :] = total.astype(BF16)
+                return
+            here = self.rows(self.offsets[level + 1], self.sizes[level + 1])
+            total = r.half[self.b, here, :].astype(F32)
+            for k in range(1, count):
+                total = total + r.slots[self.slot(level, lax.rem(index + k, count)), :].astype(F32)
+            (r.gat if last else r.half)[self.b, here, :] = total.astype(BF16)
+
+        def send(self, level):
+            if self.spread and level == len(self.axes) - 1:
+                here = self.rows(self.offsets[level], self.sizes[level])
+                r.slots[self.slot(level, self.axes[level][1]), :] = r.half[self.b, here, :]
+            self.each(level, lambda k: self.scatter(level, k).start())
+
+        def share(self, level):
+            if level:
+                self.each(level, lambda k: self.gather(level, k).start())
+                return
+            self.each(0, lambda k: self.result(k, s).start())
+
+            @pl.when(s == self.b)
+            def _():
+                self.own().start()
+
+            @pl.when(s != self.b)
+            def _():
+                self.result(0, s).start()
+
+        def plan(self):
+            depth = len(self.axes)
+            top = depth - 2 if self.spread else depth - 1
+            yield self.to_core().start()
+            self.first()
+            yield self.send(0)
+            for level in range(1, depth):
+                self.collect(level - 1)
+                yield self.send(level)
+            self.collect(depth - 1)
+            yield self.share(top)
+            for level in range(top, 0, -1):
+                self.each(level, lambda k, level=level: self.gather(level, k).wait_recv())
+                yield self.share(level - 1)
+
+            @pl.when(s == self.b)
+            def _():
+                self.own().wait()
+                self.each(0, lambda k: self.result(k, self.b).wait_recv())
+                over(0, self.axes[0][0], lambda k: self.result(k, 1 - self.b).wait_recv())
+
+            @pl.when(s != self.b)
+            def _():
+                self.result(0, s).wait_send()
+
+            self.to_core().wait_send()
+            for level in range(depth):
+                self.each(level, lambda k, level=level: self.scatter(level, k).wait_send())
+            for level in range(1, top + 1):
+                self.each(level, lambda k, level=level: self.gather(level, k).wait_send())
+            self.each(0, lambda k: self.result(k, s).wait_send())
+            yield True
+
+        def step(self):
+            return next(self.steps, True)
+
+    sums_of = [Reduced(b, which) for b in range(2) for which in (GLU, OUT, IN)]
+    by_name = dict(zip(("glu0", "out0", "in0", "glu1", "out1", "in1"), sums_of))
+
+    def go(names):
+        for name in names.split():
+            by_name[name].step()
 
     def vec_seq(b, k):
         block = r.vec_a.at[b, q]
@@ -565,6 +678,20 @@
         load_w[i].wait()
         send_w[i].wait_recv()
     load_cot.wait()
+
+    def order_cot(rows, carry):
+        r.cotv[rows, :] = mm(r.order[...], r.cotv[rows, :]).astype(BF16)
+        return carry
+
+    row_tiles(order_cot, 0)
+
+    def in_time(src, dst):
+        def tile(rows, carry):
+            dst[rows, :] = t_mm(r.order[...], src[rows, :]).astype(BF16)
+            return carry
+
+        row_tiles(tile, 0)
+
     zero_row = jnp.zeros((1, D), F32)
 
     def nothing():
@@ -583,6 +710,7 @@
 
     norm_sums(1, forward_out(0, finish_one, zero_row))
     send_all(1)
+    in_time(r.act.at[1], r.leave.at[0])
     norm_merge(1)
     forward_in(1)
     starts = carry(1, r.u.at[1], ahead1, True, nothing)
@@ -594,103 +722,98 @@
     wide_zero = jnp.zeros((1, 2 * D), F32)
     by_skip, by_bias = forward_out(1, finish_two, (zero_row, wide_zero))
 
-    keep_act = pltpu.make_async_copy(r.act.at[1 + s], r.act_out.at[s], r.local.at[5])
-    keep_act.start()
-    give_act = remote(r.act.at[1 + other], r.act_out.at[s], r.far_send.at[4], r.far_recv.at[4], sibling)
-    give_act.start()
+    keep_act = pltpu.make_async_copy(r.leave.at[s], r.act_out.at[s], r.local.at[5])
+    give_act = remote(r.leave.at[other], r.act_out.at[s], r.far_send.at[4], r.far_recv.at[4], sibling)
 
     back0, back1 = decay(0, -1.0), decay(1, -1.0)
 
     def glu_and_out(b):
         weight_grad(b, GLU, r.active[b], r.gg)
-        step_core(b, GLU)
+        go(f"glu{b}")
         weight_grad(b, OUT, r.readout[b], r.gm)
-        step_core(b, OUT)
-
-    starts = carry(2, r.adj, back1, False, lambda: glu_and_out(1))
+        go(f"out{b}")
+
+    def first_pieces():
+        glu_and_out(1)
+        in_time(r.act.at[2], r.leave.at[1])
+        keep_act.start()
+        give_act.start()
+        go("glu1 out1")
+
+    starts = carry(2, r.adj, back1, False, first_pieces)
     by_decay = fill_adjoint(1, starts, back1, False)
     put_rows(2, *back_in(1))
     send_all(2)
-    step_owner(1, GLU)
-    step_owner(1, OUT)
+    weight_grad(1, IN, r.scaled[1], r.readout.at[1])
+    go("in1")
     vec_one(1, by_skip, by_bias, by_decay)
-    weight_grad(1, IN, r.scaled[1], r.gp)
-    step_core(1, IN)
+    go(PLAN[0])
     slope, by_bias_total, by_gain_total = back_norm(2, 1)
 
     def through(rows, carry):
         live = wide(r.live[rows, :])
         upstream = r.cotv[rows, :].astype(F32)
         grad = source_grad(1, rows, upstream, live, slope, by_bias_total, by_gain_total).astype(BF16)
-        r.ig[1, rows, :] = grad
+        r.ig[rows, :] = grad
         return back_tile(0, rows, live * grad.astype(F32), r.gate[rows, :], r.steep[rows, :], carry)
 
     by_skip, by_bias = row_tiles(through, (zero_row, wide_zero))
 
     def next_pieces():
-        step_line(1, GLU)
-        step_line(1, OUT)
-        step_owner(1, IN)
+        go(PLAN[1])
+        glu_and_out(0)
+        go(PLAN[2])
         vec_two(1)
-        glu_and_out(0)
 
     starts = carry(3, r.adj, back0, True, next_pieces)
     by_decay = fill_adjoint(0, starts, back0, True)
+    go(PLAN[3])
     put_rows(3, *back_in(0))
     send_all(3)
-    weight_grad(0, IN, r.scaled[0], r.gp)
-    step_core(0, IN)
-    step_owner(0, GLU)
-    step_owner(0, OUT)
+    weight_grad(0, IN, r.scaled[0], r.readout.at[0])
+    go("in0")
     vec_one(0, by_skip, by_bias, by_decay)
-    step_line(1, IN)
-    step_result(1, GLU)
-    step_result(1, OUT)
+    go(PLAN[4])
     vec_three(1)
+    keep_act.wait()
+    give_act.wait_send()
+    in_time(r.ig, r.leave.at[1])
+    go(PLAN[5])
     slope0, by_bias_total0, by_gain_total0 = back_norm(3, 0)
 
     def last(rows, carry):
         live = wide(r.live[rows, :])
-        upstream = r.ig[1, rows, :].astype(F32)
+        upstream = r.ig[rows, :].astype(F32)
         grad = source_grad(0, rows, upstream, live, slope0, by_bias_total0, by_gain_total0)
-        r.ig[0, rows, :] = (live * grad).astype(BF16)
+        r.leave[0, rows, :] = t_mm(r.order[...], (live * grad).astype(BF16)).astype(BF16)
         return carry
 
     row_tiles(last, 0)
-    keep_ig = pltpu.make_async_copy(r.ig.at[s], r.ig_out.at[s], r.local.at[6])
+    keep_ig = pltpu.make_async_copy(r.leave.at[s], r.ig_out.at[s], r.local.at[6])
     keep_ig.start()
-    give_ig = remote(r.ig.at[other], r.ig_out.at[s], r.far_send.at[5], r.far_recv.at[5], sibling)
+    give_ig = remote(r.leave.at[other], r.ig_out.at[s], r.far_send.at[5], r.far_recv.at[5], sibling)
     give_ig.start()
 
-    step_owner(0, IN)
-    step_line(0, GLU)
-    step_line(0, OUT)
-    step_result(1, IN)
+    go(PLAN[6])
     vec_two(0)
-    step_line(0, IN)
-    step_result(0, GLU)
-    step_result(0, OUT)
+    go(PLAN[7])
     vec_three(0)
     give_vec = remote(r.vec_tot.at[other], r.vec_far, r.far_send.at[6], r.far_recv.at[6], sibling)
     give_vec.start()
-    step_result(0, IN)
+    go(PLAN[8])
     give_vec.wait_recv()
     total = r.vec_tot[s] + r.vec_far[...]
-    r.o_gain[...] = total[0:1]
-    r.o_bias[...] = total[1:2]
-    r.o_skip[...] = total[2:3]
-    r.o_bglu[:, :D] = total[3:4]
-    r.o_bglu[:, D:] = total[4:5]
+    r.small[0:5, :] = total[0:5]
     grad_re, grad_im = total[5:6, :STATES], total[5:6, STATES:]
     grad_rate = total[6:7, :STATES] * jnp.exp(-double) / scale_sq - (grad_re * decay_re + grad_im * decay_im)
-    r.o_nu[...] = grad_rate * rate
-    r.o_theta[...] = (grad_im * decay_re - grad_re * decay_im) * phase
-
-    for b in (1, 0):
-        for which in (GLU, OUT, IN):
-            step_end(b, which)
-    keep_act.wait()
-    give_act.wait()
+    r.small[5:6, :STATES] = grad_rate * rate
+    r.small[5:6, STATES:] = (grad_im * decay_re - grad_re * decay_im) * phase
+    r.small[6:8, :] = jnp.zeros((2, D), F32)
+
+    for one in (3, 4, 5, 0, 1, 2):
+        while sums_of[one].step() is not True:
+            pass
+    give_act.wait_recv()
     keep_ig.wait()
     give_ig.wait()
     give_vec.wait_send()
@@ -703,6 +826,54 @@
     for b in range(2):
         over(1, ns, lambda k, b=b: vec_seq(b, k).wait_send())
         over(1, nd, lambda k, b=b: vec_dp(b, k).wait_send())
+
+
+def results_kernel(
+    tokens, act, ig, grads, small, o_act, o_ig, o_glu, o_out, o_in, o_gain, o_bias, o_nu, o_theta, o_skip, o_bglu,
+    act_v, ig_v, ig_f, grads_v, grads_f, act_sem, ig_sem, grad_sem,
+):
+    copy = pltpu.make_async_copy
+    act_in = [copy(act.at[i], act_v.at[i], act_sem.at[i, 0]) for i in range(MICRO)]
+    ig_in = [copy(ig.at[i], ig_v.at[i], ig_sem.at[i, 0]) for i in range(MICRO)]
+    parts = [pl.ds(GRAD_AT[i], GRAD_ROWS[i]) for i in (GLU, OUT, IN)]
+    grads_in = [copy(grads.at[parts[i]], grads_v.at[parts[i]], grad_sem.at[i, 0]) for i in (GLU, OUT, IN)]
+    for one in ig_in + grads_in + act_in:
+        one.start()
+    o_gain[...] = small[0:1, :]
+    o_bias[...] = small[1:2, :]
+    o_skip[...] = small[2:3, :]
+    o_bglu[:, :D] = small[3:4, :]
+    o_bglu[:, D:] = small[4:5, :]
+    o_nu[...] = small[5:6, :STATES]
+    o_theta[...] = small[5:6, STATES:]
+    out = []
+
+    def leave(src, dst, sem):
+        out.append(copy(src, dst, sem))
+        out[-1].start()
+
+    for i in range(MICRO):
+        ig_in[i].wait()
+
+        def tile(j, carry, i=i):
+            rows = pl.ds(pl.multiple_of(j * 64, 64), 64)
+            ig_f[i, rows, :] = ig_v[i, rows, :].astype(F32)
+            return carry
+
+        lax.fori_loop(0, tokens // 64, tile, 0)
+        leave(ig_f.at[i], o_ig.at[i], ig_sem.at[i, 1])
+    for i, dst in ((GLU, o_glu), (OUT, o_out), (IN, o_in)):
+        grads_in[i].wait()
+        for c in range(GRAD_ROWS[i] // D):
+            at = GRAD_AT[i] + c * D
+            cols = slice(GRAD_AT[i] // 4 + c * LANES, GRAD_AT[i] // 4 + (c + 1) * LANES)
+            grads_f[:, cols] = grads_v[at : at + D, :].astype(F32)
+        leave(grads_f.at[:, GRAD_AT[i] // 4 : (GRAD_AT[i] + GRAD_ROWS[i]) // 4], dst, grad_sem.at[i, 1])
+    for i in range(MICRO):
+        act_in[i].wait()
+        leave(act_v.at[i], o_act.at[i], act_sem.at[i, 1])
+    for one in out:
+        one.wait()
 
 
 def body(ns, nd, inputs, mask, gain, bias, nu, theta, w_in, w_out, skip, w_glu, b_glu, cotangent):
@@ -718,12 +889,7 @@
         "act_out": jax.ShapeDtypeStruct((MICRO, tokens, D), BF16),
         "ig_out": jax.ShapeDtypeStruct((MICRO, tokens, D), BF16),
         "grads": jax.ShapeDtypeStruct((ALL_ROWS, LANES), BF16),
-        "o_gain": jax.ShapeDtypeStruct((1, D), F32),
-        "o_bias": jax.ShapeDtypeStruct((1, D), F32),
-        "o_nu": jax.ShapeDtypeStruct((1, STATES), F32),
-        "o_theta": jax.ShapeDtypeStruct((1, STATES), F32),
-        "o_skip": jax.ShapeDtypeStruct((1, D), F32),
-        "o_bglu": jax.ShapeDtypeStruct((1, 2 * D), F32),
+        "small": jax.ShapeDtypeStruct((8, D), F32),
     }
     any_out = {"act_out", "ig_out", "grads"}
     half = ALL_ROWS // 2
@@ -748,17 +914,16 @@
         "gg": vmem((tokens, 2 * D), BF16),
         "gm": vmem((tokens, D), BF16),
         "adj": vmem((4, tokens, LANES), F32),
-        "gp": vmem((tokens, D), BF16),
-        "masked": vmem((tokens, D), F32),
-        "ig": vmem((2, tokens, D), BF16),
+        "ig": vmem((tokens, D), BF16),
+        "leave": vmem((2, tokens, D), BF16),
+        "order": vmem((ROWS, ROWS), BF16),
         "bnb": vmem((4, ns * nd, 9, LANES), F32),
         "scb": vmem((4, ns, 4 * per, LANES), F32),
         "dw": vmem((2, ALL_ROWS, LANES), BF16),
         "sec": vmem((2, half, LANES), BF16),
         "half": vmem((2, half, LANES), BF16),
-        "rs": vmem((2, ns, half // ns, LANES), BF16),
-        "line": vmem((2, nd, half // ns, LANES), BF16),
-        "sum": vmem((2, half // ns, LANES), BF16),
+        "gat": vmem((2, half, LANES), BF16),
+        "slots": vmem((slot_rows(ns, nd)[-1], LANES), BF16),
         "vec_a": vmem((2, ns, 8, D), F32),
         "vec_b": vmem((2, nd, 8, D), F32),
         "vec_tot": vmem((2, 8, D), F32),
@@ -773,12 +938,10 @@
         "sc_recv": dma((4, ns)),
         "core_send": dma((6,)),
         "core_recv": dma((6,)),
-        "rs_send": dma((6, ns)),
-        "rs_recv": dma((6, ns)),
-        "line_send": dma((6, nd)),
-        "line_recv": dma((6, nd)),
-        "res_send": dma((6, ns)),
-        "res_recv": dma((6, 2 * ns)),
+        "rs_send": dma((6, 3, max(ns, nd))),
+        "rs_recv": dma((6, 3, max(ns, nd))),
+        "ag_send": dma((6, 3, max(ns, nd))),
+        "ag_recv": dma((6, 3, 2 * max(ns, nd))),
         "va_send": dma((2, ns)),
         "va_recv": dma((2, ns)),
         "vb_send": dma((2, nd)),
@@ -787,7 +950,7 @@
     in_any = pl.BlockSpec(memory_space=pl.ANY)
     in_vmem = pl.BlockSpec(memory_space=pltpu.VMEM)
     names = names_in + list(outs) + list(scratch)
-    act, ig, grads, d_gain, d_bias, d_nu, d_theta, d_skip, d_bglu = pl.pallas_call(
+    act, ig, grads, small = pl.pallas_call(
         functools.partial(kernel, ns, nd, per, span, names),
         out_shape=list(outs.values()),
         in_specs=[in_any if name in any_in else in_vmem for name in names_in],
@@ -811,22 +974,38 @@
         w_glu,
     )
 
-    def matrix(which):
-        part = grads[GRAD_AT[which] : GRAD_AT[which] + GRAD_ROWS[which]].reshape(-1, D, LANES)
-        return jnp.transpose(part, (1, 0, 2)).reshape(1, D, -1).astype(F32)
-
+    wide_out = [(1, D), (1, D), (1, STATES), (1, STATES), (1, D), (1, 2 * D)]
+    big_out = [((MICRO, tokens, D), BF16), ((MICRO, tokens, D), F32)]
+    big_out += [((D, GRAD_ROWS[which] // 4), F32) for which in (GLU, OUT, IN)]
+    act, ig, d_glu, d_out, d_in, d_gain, d_bias, d_nu, d_theta, d_skip, d_bglu = pl.pallas_call(
+        functools.partial(results_kernel, tokens),
+        out_shape=[jax.ShapeDtypeStruct(*x) for x in big_out] + [jax.ShapeDtypeStruct(x, F32) for x in wide_out],
+        in_specs=[in_any] * 3 + [in_vmem],
+        out_specs=[in_any] * 5 + [in_vmem] * 6,
+        scratch_shapes=[
+            vmem((MICRO, tokens, D), BF16),
+            vmem((MICRO, tokens, D), BF16),
+            vmem((MICRO, tokens, D), F32),
+            vmem((ALL_ROWS, LANES), BF16),
+            vmem((D, ALL_ROWS // 4), F32),
+            dma((2, 2)),
+            dma((2, 2)),
+            dma((3, 2)),
+        ],
+        compiler_params=pltpu.CompilerParams(vmem_limit_bytes=60 * 2**20),
+    )(act, ig, grads, small)
     whole = (1, MICRO * per, span, D)
     return (
         act.reshape(whole),
-        ig.reshape(whole).astype(F32),
+        ig.reshape(whole),
         d_gain,
         d_bias,
         d_nu,
         d_theta,
-        matrix(IN),
-        matrix(OUT),
+        d_in[None],
+        d_out[None],
         d_skip,
-        matrix(GLU),
+        d_glu[None],
         d_bglu,
     )
 

time: 146 us -> 116 us (0.79)
  local copies, waits for them, and re-layouts: 13.6 us -> 0 us
  Pallas kernels: 127 us -> 115 us
  other arithmetic: 4.62 us -> 0 us
    pallas_call x1, Pallas kernels: 127 us -> 108 us  [body(): pl.pallas_call(functools.partial(kernel, ns, nd, per, span, names), out_s...]
    pallas_call x0 -> x1, Pallas kernels: none -> 7.21 us  [body(): pl.pallas_call(functools.partial(results_kernel, tokens), out_shape=[jax....]
    convert_element_type x6 -> x0, local copies, waits for them, and re-layouts: 6.84 us -> none  [matrix(): return jnp.transpose(part, (1, 0, 2)).reshape(1, D, -1).astype(F32)]
    unnamed x23 -> x0, local copies, waits for them, and re-layouts: 5.25 us -> none
    convert_element_type x4 -> x0, other arithmetic: 4.62 us -> none  [the longest x1 4.35 us: body(): ig.reshape(whole).astype(F32)]
    slice x2 -> x0, local copies, waits for them, and re-layouts: 1.51 us -> none  [matrix(): grads[GRAD_AT[which]:GRAD_AT[which] + GRAD_ROWS[which]]]
where the time goes in v1:
time: 116 us
  Pallas kernels  115 us (99%)
    pallas_call x1, Pallas kernels, body(): pl.pallas_call(functools.partial(kernel, ns, nd, per, span, names), out_s...  108 us
    pallas_call x1, Pallas kernels, body(): pl.pallas_call(functools.partial(results_kernel, tokens), out_shape=[jax....  7.21 us

profile of v1, /device:TPU:0, one launch (start us, length us, event | category | flops | bytes accessed | tf_op | source)
XLA Modules:
  0.0 116.1 jit_solution(918053426760165785)
XLA Ops:
  0.6 108.2 %shard_map.203 = (bf16[2,1024,512]{2,1,0:T(8,128)(2,1)}, bf16[2,1024,512]{2,1,0:T(8,128)(2,1)}, bf16[8192,128]{1,0:T(8,128)(2,1)}, f32[8,512]{1,0:T(8,128)}) custom-call(bf16[2,1024,512]{2,1,0:T(8,128)(2,1)} %refs_0_.1, bf16[2,1024,512]{2,1,0:T(8,128)(2,1)} %refs_1_.1, s32[2,1024]{1,0:T(2,128)} %refs_2_.1, f32[1,512]{1,0:T(1,128)} %refs_3_.1, ...), custom_call_target="tpu_custom_call" | custom-call | tf_op jit(solution)/shard_map/pallas_call | solution.py:953
  108.9 7.2 %shard_map.204 = (bf16[2,1024,512]{2,1,0:T(8,128)(2,1)}, f32[2,1024,512]{2,1,0:T(8,128)}, f32[512,1024]{1,0:T(8,128)}, f32[512,512]{1,0:T(8,128)}, f32[512,512]{...) custom-call(bf16[2,1024,512]{2,1,0:T(8,128)(2,1)} %get-tuple-element, ...), custom_call_target="tpu_custom_call" | custom-call | tf_op jit(solution)/shard_map/pallas_call | solution.py:980

commit v2 on v1

--- a/solution.py
+++ b/solution.py
@@ -21,18 +21,29 @@
 GRAD_ROWS = (4096, 2048, 2048)
 GRAD_AT = (0, 4096, 6144)
 ALL_ROWS = 8192
-ORDERS = (("seq", "dp"), ("seq", "dp"), ("seq", "dp"), ("seq", "dp"), ("seq", "dp"), ("seq", "dp"))
-PLAN = (
-    "in1",
-    "glu1 out1",
-    "in1",
-    "glu0 out0",
-    "in0 glu1 out1 in1",
-    "",
-    "glu1 out1 in1 glu0 out0",
-    "in0 glu0 out0",
-    "in0 glu0 out0 in0",
+SD = ("seq", "dp")
+DS = ("dp", "seq")
+PARTS = (
+    ((0, 2048, SD), (2048, 2048, SD),),
+    ((0, 2048, SD),),
+    ((0, 1024, SD), (1024, 1024, DS),),
+    ((0, 4096, SD),),
+    ((0, 2048, SD),),
+    ((0, 1024, SD), (1024, 1024, DS),),
 )
+FLAT = tuple((n, *part) for n, parts in enumerate(PARTS) for part in parts)
+DEPTH = max(len(part[-1]) for part in FLAT)
+PLAN = {
+    "carry two": (104, 103, 6),
+    "filled two": (),
+    "norm two": (5, 105, 6, 7, 8),
+    "through": (),
+    "carry one": (200, 100, 6, 5, 7),
+    "filled one": (0, 8, 1, 102),
+    "norm one": (3, 101, 4, 6, 2, 5, 0, 8, 7),
+    "last": (201, 1, 4, 3),
+    "end": (5, 0, 2, 4, 3, 1, 7, 8, 0, 2, 3, 202, 4, 1, 2),
+}
 ROOT = math.sqrt(2.0 / math.pi)
 CUBE = 0.044715
 
@@ -94,11 +105,10 @@
     inner = next(n for n in range(math.isqrt(ns), 0, -1) if ns % n == 0)
     sizes = {"seq": ns, "dp": nd, "in": inner, "out": ns // inner}
     bases = [0]
-    for n, order in enumerate(ORDERS):
-        rows = GRAD_ROWS[n % 3] // 2
+    for _, _, rows, order in FLAT:
         counts = [sizes[name] for name in order]
-        spread = rows // math.prod(counts) % 16 != 0
-        start, size = slots_of(rows, counts, spread)[-1]
+        spread = rows // 2 // math.prod(counts) % 16 != 0
+        start, size = slots_of(rows // 2, counts, spread)[-1]
         bases.append(bases[-1] + start + counts[-1] * size)
     return bases
 
@@ -136,11 +146,33 @@
     def over(low, high, body):
         lax.fori_loop(low, high, lambda k, c: (body(k), c)[1], 0)
 
+    arriving = {}
+    leaving = {}
+
+    def begin(key, start, whole):
+        start()
+        arriving[key] = leaving[key] = whole
+
+    def arrive(key):
+        arriving.pop(key).wait_recv()
+
+    def leave(key):
+        leaving.pop(key).wait_send()
+
+    def end_all():
+        for key in list(arriving):
+            arrive(key)
+        for key in list(leaving):
+            leave(key)
+
+    def alone(key, copy):
+        begin(key, copy.start, copy)
+
     def row_tiles(body, init):
         def step(i, carry):
             return body(pl.ds(pl.multiple_of(i * ROWS, ROWS), ROWS), carry)
 
-        return lax.fori_loop(0, tiles, step, init)
+        return lax.fori_loop(0, tiles, step, init, unroll=4)
 
     slot_base = slot_rows(ns, nd)
 
@@ -187,20 +219,18 @@
 
     count = jnp.zeros((1, 1), F32)
     row = lax.broadcasted_iota(jnp.int32, (tokens, LANES), 0)
-    inside = lax.rem(row, ROWS)
-    token = row - inside + lax.rem(inside, EIGHT) * SEG + inside // EIGHT
-    step_of = lax.rem(token, span)
-    sequence = token // span
-    ends_at = jnp.zeros((tokens, LANES), jnp.int32)
+    token = (row & -ROWS) + (row & (EIGHT - 1)) * SEG + ((row & (ROWS - 1)) >> (EIGHT.bit_length() - 1))
+    live = jnp.zeros((tokens, LANES), F32)
     for i in range(per):
         here = jnp.sum(r.mask[pl.ds(s * per + i, 1), :], axis=1, keepdims=True)
-        ends_at = jnp.where(sequence == i, here, ends_at)
+        live = jnp.where((token >= i * span) & (token < i * span + here), 1.0, live)
         count = count + here.astype(F32)
-    r.live[...] = jnp.where(step_of < ends_at, 1.0, 0.0)
+    r.live[...] = live
     count_row = jnp.broadcast_to(count, (1, LANES))
     to_row = lax.broadcasted_iota(jnp.int32, (ROWS, ROWS), 0)
     from_row = lax.broadcasted_iota(jnp.int32, (ROWS, ROWS), 1)
-    r.order[...] = jnp.where(from_row == lax.rem(to_row, EIGHT) * SEG + to_row // EIGHT, 1.0, 0.0).astype(BF16)
+    came_from = (to_row & (EIGHT - 1)) * SEG + (to_row >> (EIGHT.bit_length() - 1))
+    r.order[...] = jnp.where(from_row == came_from, 1.0, 0.0).astype(BF16)
     load_x.wait()
 
     def mask_input(rows, total):
@@ -223,13 +253,15 @@
 
     def to_all(ph, k):
         block = r.bnb.at[ph, me]
-        return remote(block, block, r.bn_send.at[ph, k], r.bn_recv.at[ph, k], any_peer(k))
+        return remote(block, block, r.bn_send.at[ph], r.bn_recv.at[ph], any_peer(k))
 
     def send_all(ph):
-        over(1, peers, lambda k: to_all(ph, k).start())
+        blocks = r.bnb.at[ph, pl.ds(0, peers - 1)]
+        whole = remote(blocks, blocks, r.bn_send.at[ph], r.bn_recv.at[ph], sibling)
+        begin(("all", ph), lambda: over(1, peers, lambda k: to_all(ph, k).start()), whole)
 
     def wait_all(ph):
-        over(1, peers, lambda k: to_all(ph, k).wait_recv())
+        arrive(("all", ph))
 
     def norm_sums(b, total):
         mean = total / jnp.maximum(wide(count_row), 1.0)
@@ -252,13 +284,14 @@
     pl.semaphore_wait(barrier, peers + ns - 1 + nd - 1)
     send_all(0)
     send_prm = remote(r.prm.at[s], r.prm.at[s], r.far_send.at[0], r.far_recv.at[0], sibling)
-    send_prm.start()
     send_w = [
         remote(src.at[0], dst.at[s], r.far_send.at[1 + i], r.far_recv.at[1 + i], sibling)
         for i, (src, dst) in enumerate(weights)
     ]
-    for copy in send_w:
-        copy.start()
+
+    alone("prm", send_prm)
+    for i, copy in enumerate(send_w):
+        alone(("w", i), copy)
 
     def decay(b, sign):
         out = []
@@ -303,7 +336,7 @@
 
     def to_seq(ph, k):
         block = r.scb.at[ph, q]
-        return remote(block, block, r.sc_send.at[ph, k], r.sc_recv.at[ph, k], seq_peer(k))
+        return remote(block, block, r.sc_send.at[ph], r.sc_recv.at[ph], seq_peer(k))
 
     def carry(ph, drive, a, reverse, between):
         def step(i, states):
@@ -321,11 +354,13 @@
             for c in range(2):
                 r.scb[ph, q, 4 * i + c : 4 * i + c + 1, :] = sums[c][0][last : last + 1]
                 r.scb[ph, q, 4 * i + 2 + c : 4 * i + 3 + c, :] = sums[c][1][last : last + 1]
-        over(1, ns, lambda k: to_seq(ph, k).start())
+        ends_of = r.scb.at[ph, pl.ds(0, ns - 1)]
+        whole = remote(ends_of, ends_of, r.sc_send.at[ph], r.sc_recv.at[ph], sibling)
+        begin(("seq", ph), lambda: over(1, ns, lambda k: to_seq(ph, k).start()), whole)
         first = jnp.where(place == (nseg - 1 if reverse else 0), 1.0, 0.0)
         reach = [seg_scan(first, zero, jumps[c], reverse) for c in range(2)]
         between()
-        over(1, ns, lambda k: to_seq(ph, k).wait_recv())
+        arrive(("seq", ph))
         starts = []
         for c in range(2):
             far = power(*a[c], span)
@@ -451,13 +486,21 @@
     def normed(b, rows):
         return (r.act[b, rows, :].astype(F32) - r.stat[b, 0:1, :]) * r.stat[b, 1:2, :]
 
+    projected_grads = (r.cotv, r.ig)
+
+    def round_adjoint(b):
+        def tile(rows, carry):
+            adjoint = jnp.concatenate([r.adj[c, rows, :] for c in range(4)], axis=1)
+            projected_grads[b][rows, :] = adjoint.astype(BF16)
+            return carry
+
+        row_tiles(tile, 0)
+
     def back_in(b):
         skip = r.prm[b, 2:3, :]
 
         def tile(rows, carry):
-            grad_projected = jnp.concatenate([r.adj[c, rows, :] for c in range(4)], axis=1).astype(BF16)
-            r.readout[b, rows, :] = grad_projected
-            grad_scaled = skip * r.gm[rows, :].astype(F32) + mm_t(grad_projected, r.win[b])
+            grad_scaled = skip * r.gm[rows, :].astype(F32) + mm_t(projected_grads[b][rows, :], r.win[b])
             masked = wide(r.live[rows, :]) * grad_scaled
             r.slope[b, rows, :] = masked
             return carry[0] + column_sum(masked * normed(b, rows)), carry[1] + column_sum(masked)
@@ -489,7 +532,7 @@
             r.dw[b, pl.ds(at + 512, 512), :] = grad[:, LANES:]
             return carry
 
-        lax.fori_loop(0, columns // 256, tile, 0)
+        lax.fori_loop(0, columns // 256, tile, 0, unroll=2)
 
     inner = next(n for n in range(math.isqrt(ns), 0, -1) if ns % n == 0)
     outer = ns // inner
@@ -501,17 +544,20 @@
         "out": (outer, q_out, lambda k: {"seq": lax.rem(q_out + k, outer) * inner + q_in}),
     }
 
+    results = []
+
     class Reduced:
-        def __init__(self, b, which):
-            self.b, self.n, self.at = b, b * 3 + which, GRAD_AT[which]
+        def __init__(self, n):
+            which, start, rows, order = FLAT[n]
+            self.b, self.n, self.at = which // 3, n, GRAD_AT[which % 3] + start
             self.base = self.at // 2
-            self.axes = [axes[name] for name in ORDERS[self.n]]
-            self.sizes, self.offsets = [GRAD_ROWS[which] // 2], [0]
+            self.axes = [axes[name] for name in order]
+            self.sizes, self.offsets = [rows // 2], [0]
             for count, index, _ in self.axes:
                 self.sizes.append(self.sizes[-1] // count)
                 self.offsets.append(self.offsets[-1] + index * self.sizes[-1])
             self.spread = self.sizes[-1] % 16 != 0
-            self.slots = slots_of(GRAD_ROWS[which] // 2, [count for count, _, _ in self.axes], self.spread)
+            self.slots = slots_of(rows // 2, [count for count, _, _ in self.axes], self.spread)
             self.slot_base = slot_base[self.n]
             self.steps = self.plan()
 
@@ -535,39 +581,43 @@
                 size = self.sizes[level + 1]
                 src = r.half.at[self.b, self.rows(self.offsets[level] + lax.rem(index + k, count) * size, size)]
             dst = r.slots.at[self.slot(level, index)]
-            return remote(src, dst, r.rs_send.at[self.n, level, k], r.rs_recv.at[self.n, level, k], peer(k))
+            return remote(src, dst, r.rs_send.at[self.n, level], r.rs_recv.at[self.n, level], peer(k))
 
         def gather(self, level, k):
             block = r.gat.at[self.b, self.rows(self.offsets[level + 1], self.sizes[level + 1])]
-            return remote(
-                block, block, r.ag_send.at[self.n, level, k], r.ag_recv.at[self.n, level, k], self.axes[level][2](k)
-            )
+            return remote(block, block, r.ag_send.at[self.n, level], r.ag_recv.at[self.n, level], self.axes[level][2](k))
 
         def place(self):
             return pl.ds(pl.multiple_of(self.at + s * self.sizes[0] + self.offsets[1], 16), self.sizes[1])
 
-        def result(self, k, section):
+        def result(self, device, send):
             src = r.gat.at[self.b, self.rows(self.offsets[1], self.sizes[1])]
-            recv = r.ag_recv.at[self.n, 0, section * self.axes[0][0] + k]
-            target = {"section": self.b, **self.axes[0][2](k)} if not isinstance(k, int) or k else {"section": self.b}
-            return remote(src, r.grads.at[self.place()], r.ag_send.at[self.n, 0, k], recv, target)
+            target = {"section": self.b, **device}
+            return remote(src, r.grads.at[self.place()], send, r.ag_recv.at[self.n, 0], target)
+
+        def results_whole(self, parts):
+            rows = r.grads.at[pl.ds(0, parts * self.sizes[1])]
+            return remote(rows, rows, r.ag_send.at[self.n, 0], r.ag_recv.at[self.n, 0], sibling)
 
         def own(self):
             src = r.gat.at[self.b, self.rows(self.offsets[1], self.sizes[1])]
             return pltpu.make_async_copy(src, r.grads.at[self.place()], r.own.at[self.n])
 
+        def across(self):
+            return self.result({}, r.own.at[self.n])
+
         def each(self, level, body):
             over(1, self.axes[level][0], body)
 
         def first(self):
             size = self.sizes[0]
-            self.to_core().wait_recv()
+            arrive((self.n, "core"))
             mine = r.dw[self.b, pl.ds(pl.multiple_of(self.at + s * size, 16), size), :].astype(F32)
             there = r.sec[self.b, self.base : self.base + size, :].astype(F32)
             r.half[self.b, self.base : self.base + size, :] = (mine + there).astype(BF16)
 
         def collect(self, level):
-            self.each(level, lambda k: self.scatter(level, k).wait_recv())
+            arrive((self.n, "scatter", level))
             count, index, _ = self.axes[level]
             last = level == len(self.axes) - 1
             if self.spread and last:
@@ -584,13 +634,19 @@
             if self.spread and level == len(self.axes) - 1:
                 here = self.rows(self.offsets[level], self.sizes[level])
                 r.slots[self.slot(level, self.axes[level][1]), :] = r.half[self.b, here, :]
-            self.each(level, lambda k: self.scatter(level, k).start())
+            start, size = self.slots[level]
+            rows = r.slots.at[pl.ds(self.slot_base + start, (self.axes[level][0] - 1) * size)]
+            whole = remote(rows, rows, r.rs_send.at[self.n, level], r.rs_recv.at[self.n, level], sibling)
+            begin((self.n, "scatter", level), lambda: self.each(level, lambda k: self.scatter(level, k).start()), whole)
 
         def share(self, level):
+            count, _, peer = self.axes[level]
             if level:
-                self.each(level, lambda k: self.gather(level, k).start())
+                rows = r.gat.at[self.b, pl.ds(self.base, (count - 1) * self.sizes[level + 1])]
+                whole = remote(rows, rows, r.ag_send.at[self.n, level], r.ag_recv.at[self.n, level], sibling)
+                begin((self.n, "gather", level), lambda: self.each(level, lambda k: self.gather(level, k).start()), whole)
                 return
-            self.each(0, lambda k: self.result(k, s).start())
+            self.each(0, lambda k: self.result(peer(k), r.ag_send.at[self.n, 0]).start())
 
             @pl.when(s == self.b)
             def _():
@@ -598,12 +654,29 @@
 
             @pl.when(s != self.b)
             def _():
-                self.result(0, s).start()
+                self.across().start()
+
+            results.append(self)
+
+        def finish(self):
+            count = self.axes[0][0]
+
+            @pl.when(s == self.b)
+            def _():
+                self.own().wait()
+                self.results_whole(2 * count - 1).wait_recv()
+
+            @pl.when(s != self.b)
+            def _():
+                self.across().wait_send()
+
+            if count > 1:
+                self.results_whole(count - 1).wait_send()
 
         def plan(self):
             depth = len(self.axes)
             top = depth - 2 if self.spread else depth - 1
-            yield self.to_core().start()
+            yield alone((self.n, "core"), self.to_core())
             self.first()
             yield self.send(0)
             for level in range(1, depth):
@@ -612,44 +685,38 @@
             self.collect(depth - 1)
             yield self.share(top)
             for level in range(top, 0, -1):
-                self.each(level, lambda k, level=level: self.gather(level, k).wait_recv())
+                arrive((self.n, "gather", level))
                 yield self.share(level - 1)
-
-            @pl.when(s == self.b)
-            def _():
-                self.own().wait()
-                self.each(0, lambda k: self.result(k, self.b).wait_recv())
-                over(0, self.axes[0][0], lambda k: self.result(k, 1 - self.b).wait_recv())
-
-            @pl.when(s != self.b)
-            def _():
-                self.result(0, s).wait_send()
-
-            self.to_core().wait_send()
-            for level in range(depth):
-                self.each(level, lambda k, level=level: self.scatter(level, k).wait_send())
-            for level in range(1, top + 1):
-                self.each(level, lambda k, level=level: self.gather(level, k).wait_send())
-            self.each(0, lambda k: self.result(k, s).wait_send())
-            yield True
 
         def step(self):
             return next(self.steps, True)
 
-    sums_of = [Reduced(b, which) for b in range(2) for which in (GLU, OUT, IN)]
-    by_name = dict(zip(("glu0", "out0", "in0", "glu1", "out1", "in1"), sums_of))
-
-    def go(names):
-        for name in names.split():
-            by_name[name].step()
+    sums_of = [Reduced(n) for n in range(len(FLAT))]
+
+    factors = ((r.active, (r.gg, r.gg)), (r.readout, (r.gm, r.gm)), (r.scaled, projected_grads))
+
+    def go(gap):
+        for n in PLAN[gap]:
+            if n < 100:
+                sums_of[n].step()
+                continue
+            if n >= 200:
+                vec_steps[n - 200]()
+                continue
+            b, which = (n - 100) // 3, (n - 100) % 3
+            left, right = factors[which]
+            weight_grad(b, which, left[b], right[b])
+            for one, part in zip(sums_of, FLAT):
+                if part[0] == n - 100:
+                    one.step()
 
     def vec_seq(b, k):
         block = r.vec_a.at[b, q]
-        return remote(block, block, r.va_send.at[b, k], r.va_recv.at[b, k], seq_peer(k))
+        return remote(block, block, r.va_send.at[b], r.va_recv.at[b], seq_peer(k))
 
     def vec_dp(b, k):
         block = r.vec_b.at[b, d]
-        return remote(block, block, r.vb_send.at[b, k], r.vb_recv.at[b, k], dp_peer(k))
+        return remote(block, block, r.vb_send.at[b], r.vb_recv.at[b], dp_peer(k))
 
     def vec_one(b, by_skip, by_bias, by_decay):
         zero = jnp.zeros((1, D), F32)
@@ -661,22 +728,33 @@
         r.vec_a[b, q, 5:6, :] = jnp.concatenate([by_decay[0], by_decay[1]], axis=1)
         r.vec_a[b, q, 6:7, :] = jnp.concatenate([by_decay[2], by_decay[2]], axis=1)
         r.vec_a[b, q, 7:8, :] = zero
-        over(1, ns, lambda k: vec_seq(b, k).start())
+        rows = r.vec_a.at[b, pl.ds(0, ns - 1)]
+        whole = remote(rows, rows, r.va_send.at[b], r.va_recv.at[b], sibling)
+        begin(("vec_seq", b), lambda: over(1, ns, lambda k: vec_seq(b, k).start()), whole)
 
     def vec_two(b):
-        over(1, ns, lambda k: vec_seq(b, k).wait_recv())
+        arrive(("vec_seq", b))
         r.vec_b[b, d] = jnp.sum(r.vec_a[b], axis=0)
-        over(1, nd, lambda k: vec_dp(b, k).start())
+        rows = r.vec_b.at[b, pl.ds(0, nd - 1)]
+        whole = remote(rows, rows, r.vb_send.at[b], r.vb_recv.at[b], sibling)
+        begin(("vec_dp", b), lambda: over(1, nd, lambda k: vec_dp(b, k).start()), whole)
 
     def vec_three(b):
-        over(1, nd, lambda k: vec_dp(b, k).wait_recv())
+        arrive(("vec_dp", b))
         total = jnp.sum(r.vec_b[b], axis=0)
         r.vec_tot[b, 2:8, :] = total[2:8]
 
-    send_prm.wait_recv()
+    def vec_last():
+        vec_three(1)
+        vec_three(0)
+        alone("vec", remote(r.vec_tot.at[other], r.vec_far, r.far_send.at[6], r.far_recv.at[6], sibling))
+
+    vec_steps = (lambda: vec_two(1), lambda: vec_two(0), vec_last)
+
+    arrive("prm")
     for i in range(3):
         load_w[i].wait()
-        send_w[i].wait_recv()
+        arrive(("w", i))
     load_cot.wait()
 
     def order_cot(rows, carry):
@@ -727,27 +805,20 @@
 
     back0, back1 = decay(0, -1.0), decay(1, -1.0)
 
-    def glu_and_out(b):
-        weight_grad(b, GLU, r.active[b], r.gg)
-        go(f"glu{b}")
-        weight_grad(b, OUT, r.readout[b], r.gm)
-        go(f"out{b}")
-
     def first_pieces():
-        glu_and_out(1)
+        go("carry two")
         in_time(r.act.at[2], r.leave.at[1])
         keep_act.start()
-        give_act.start()
-        go("glu1 out1")
+        alone("act", give_act)
 
     starts = carry(2, r.adj, back1, False, first_pieces)
     by_decay = fill_adjoint(1, starts, back1, False)
+    round_adjoint(1)
+    go("filled two")
     put_rows(2, *back_in(1))
     send_all(2)
-    weight_grad(1, IN, r.scaled[1], r.readout.at[1])
-    go("in1")
     vec_one(1, by_skip, by_bias, by_decay)
-    go(PLAN[0])
+    go("norm two")
     slope, by_bias_total, by_gain_total = back_norm(2, 1)
 
     def through(rows, carry):
@@ -758,27 +829,22 @@
         return back_tile(0, rows, live * grad.astype(F32), r.gate[rows, :], r.steep[rows, :], carry)
 
     by_skip, by_bias = row_tiles(through, (zero_row, wide_zero))
+    go("through")
 
     def next_pieces():
-        go(PLAN[1])
-        glu_and_out(0)
-        go(PLAN[2])
-        vec_two(1)
+        go("carry one")
 
     starts = carry(3, r.adj, back0, True, next_pieces)
     by_decay = fill_adjoint(0, starts, back0, True)
-    go(PLAN[3])
+    round_adjoint(0)
+    go("filled one")
     put_rows(3, *back_in(0))
     send_all(3)
-    weight_grad(0, IN, r.scaled[0], r.readout.at[0])
-    go("in0")
     vec_one(0, by_skip, by_bias, by_decay)
-    go(PLAN[4])
-    vec_three(1)
+    go("norm one")
     keep_act.wait()
-    give_act.wait_send()
+    leave("act")
     in_time(r.ig, r.leave.at[1])
-    go(PLAN[5])
     slope0, by_bias_total0, by_gain_total0 = back_norm(3, 0)
 
     def last(rows, carry):
@@ -792,16 +858,13 @@
     keep_ig = pltpu.make_async_copy(r.leave.at[s], r.ig_out.at[s], r.local.at[6])
     keep_ig.start()
     give_ig = remote(r.leave.at[other], r.ig_out.at[s], r.far_send.at[5], r.far_recv.at[5], sibling)
-    give_ig.start()
-
-    go(PLAN[6])
-    vec_two(0)
-    go(PLAN[7])
-    vec_three(0)
-    give_vec = remote(r.vec_tot.at[other], r.vec_far, r.far_send.at[6], r.far_recv.at[6], sibling)
-    give_vec.start()
-    go(PLAN[8])
-    give_vec.wait_recv()
+    alone("ig", give_ig)
+
+    go("last")
+    go("end")
+    while not all([one.step() is True for one in sums_of]):
+        pass
+    arrive("vec")
     total = r.vec_tot[s] + r.vec_far[...]
     r.small[0:5, :] = total[0:5]
     grad_re, grad_im = total[5:6, :STATES], total[5:6, STATES:]
@@ -810,22 +873,10 @@
     r.small[5:6, STATES:] = (grad_im * decay_re - grad_re * decay_im) * phase
     r.small[6:8, :] = jnp.zeros((2, D), F32)
 
-    for one in (3, 4, 5, 0, 1, 2):
-        while sums_of[one].step() is not True:
-            pass
-    give_act.wait_recv()
     keep_ig.wait()
-    give_ig.wait()
-    give_vec.wait_send()
-    send_prm.wait_send()
-    for copy in send_w:
-        copy.wait_send()
-    for ph in range(4):
-        over(1, peers, lambda k, ph=ph: to_all(ph, k).wait_send())
-        over(1, ns, lambda k, ph=ph: to_seq(ph, k).wait_send())
-    for b in range(2):
-        over(1, ns, lambda k, b=b: vec_seq(b, k).wait_send())
-        over(1, nd, lambda k, b=b: vec_dp(b, k).wait_send())
+    for one in results:
+        one.finish()
+    end_all()
 
 
 def results_kernel(
@@ -929,23 +980,23 @@
         "vec_tot": vmem((2, 8, D), F32),
         "vec_far": vmem((8, D), F32),
         "local": dma((7,)),
-        "own": dma((6,)),
+        "own": dma((len(FLAT),)),
         "far_send": dma((7,)),
         "far_recv": dma((7,)),
-        "bn_send": dma((4, ns * nd)),
-        "bn_recv": dma((4, ns * nd)),
-        "sc_send": dma((4, ns)),
-        "sc_recv": dma((4, ns)),
-        "core_send": dma((6,)),
-        "core_recv": dma((6,)),
-        "rs_send": dma((6, 3, max(ns, nd))),
-        "rs_recv": dma((6, 3, max(ns, nd))),
-        "ag_send": dma((6, 3, max(ns, nd))),
-        "ag_recv": dma((6, 3, 2 * max(ns, nd))),
-        "va_send": dma((2, ns)),
-        "va_recv": dma((2, ns)),
-        "vb_send": dma((2, nd)),
-        "vb_recv": dma((2, nd)),
+        "bn_send": dma((4,)),
+        "bn_recv": dma((4,)),
+        "sc_send": dma((4,)),
+        "sc_recv": dma((4,)),
+        "core_send": dma((len(FLAT),)),
+        "core_recv": dma((len(FLAT),)),
+        "rs_send": dma((len(FLAT), DEPTH)),
+        "rs_recv": dma((len(FLAT), DEPTH)),
+        "ag_send": dma((len(FLAT), DEPTH)),
+        "ag_recv": dma((len(FLAT), DEPTH)),
+        "va_send": dma((2,)),
+        "va_recv": dma((2,)),
+        "vb_send": dma((2,)),
+        "vb_recv": dma((2,)),
     }
     in_any = pl.BlockSpec(memory_space=pl.ANY)
     in_vmem = pl.BlockSpec(memory_space=pltpu.VMEM)

time: 116 us -> 98.7 us (0.85)
  Pallas kernels: 115 us -> 97.5 us
    pallas_call x1, Pallas kernels: 108 us -> 90.3 us  [body(): pl.pallas_call(functools.partial(kernel, ns, nd, per, span, names), out_s...]
where the time goes in v2:
time: 98.7 us; the launch traced here: 98.4 us
  Pallas kernels  97.5 us (99%)
    pallas_call x1, Pallas kernels, body(): pl.pallas_call(functools.partial(kernel, ns, nd, per, span, names), out_s...  90.3 us
    pallas_call x1, Pallas kernels, body(): pl.pallas_call(functools.partial(results_kernel, tokens), out_shape=[jax....  7.21 us

profile of v2, /device:TPU:0, one launch (start us, length us, event | category | flops | bytes accessed | tf_op | source)
XLA Modules:
  0.0 98.4 jit_solution(15584578384987168495)
XLA Ops:
  0.6 90.3 %shard_map.203 = (bf16[2,1024,512]{2,1,0:T(8,128)(2,1)}, bf16[2,1024,512]{2,1,0:T(8,128)(2,1)}, bf16[8192,128]{1,0:T(8,128)(2,1)}, f32[8,512]{1,0:T(8,128)}) custom-call(bf16[2,1024,512]{2,1,0:T(8,128)(2,1)} %refs_0_.1, bf16[2,1024,512]{2,1,0:T(8,128)(2,1)} %refs_1_.1, s32[2,1024]{1,0:T(2,128)} %refs_2_.1, f32[1,512]{1,0:T(1,128)} %refs_3_.1, ...), custom_call_target="tpu_custom_call" | custom-call | tf_op jit(solution)/shard_map/pallas_call | solution.py:1004
  91.0 7.2 %shard_map.204 = (bf16[2,1024,512]{2,1,0:T(8,128)(2,1)}, f32[2,1024,512]{2,1,0:T(8,128)}, f32[512,1024]{1,0:T(8,128)}, f32[512,512]{1,0:T(8,128)}, f32[512,512]{...) custom-call(bf16[2,1024,512]{2,1,0:T(8,128)(2,1)} %get-tuple-element, ...), custom_call_target="tpu_custom_call" | custom-call | tf_op jit(solution)/shard_map/pallas_call | solution.py:1031

commit v3 on v2

--- a/solution.py
+++ b/solution.py
@@ -24,25 +24,25 @@
 SD = ("seq", "dp")
 DS = ("dp", "seq")
 PARTS = (
-    ((0, 2048, SD), (2048, 2048, SD),),
+    ((0, 1536, SD), (1536, 1536, SD), (3072, 1024, DS),),
+    ((0, 1024, SD), (1024, 1024, DS),),
     ((0, 2048, SD),),
-    ((0, 1024, SD), (1024, 1024, DS),),
     ((0, 4096, SD),),
     ((0, 2048, SD),),
-    ((0, 1024, SD), (1024, 1024, DS),),
+    ((0, 1536, SD), (1536, 512, DS),),
 )
 FLAT = tuple((n, *part) for n, parts in enumerate(PARTS) for part in parts)
 DEPTH = max(len(part[-1]) for part in FLAT)
 PLAN = {
-    "carry two": (104, 103, 6),
+    "carry two": (104, 103, 7),
     "filled two": (),
-    "norm two": (5, 105, 6, 7, 8),
-    "through": (),
-    "carry one": (200, 100, 6, 5, 7),
-    "filled one": (0, 8, 1, 102),
-    "norm one": (3, 101, 4, 6, 2, 5, 0, 8, 7),
-    "last": (201, 1, 4, 3),
-    "end": (5, 0, 2, 4, 3, 1, 7, 8, 0, 2, 3, 202, 4, 1, 2),
+    "norm two": (105, 6, 7, 8, 9),
+    "through": (7,),
+    "carry one": (200, 100, 6, 7, 101, 8),
+    "filled one": (3, 2, 9),
+    "norm one": (0, 102, 1, 8, 3, 2, 6, 5),
+    "last": (8, 1, 9, 0, 6, 201),
+    "end": (4, 0, 5, 4, 3, 1, 2, 0, 5, 2, 4, 1, 202, 4, 9, 3, 5),
 }
 ROOT = math.sqrt(2.0 / math.pi)
 CUBE = 0.044715
@@ -176,13 +176,31 @@
 
     slot_base = slot_rows(ns, nd)
 
+    def skewed(tile, sums):
+        waiting, running = [pl.ds(i * ROWS, ROWS) for i in range(tiles)], []
+        while waiting or running:
+            if waiting:
+                running.append(tile(waiting.pop(0), sums))
+            running = [one for one in running if next(one, True) is not True]
+        return sums
+
     barrier = pltpu.get_barrier_semaphore()
 
     def greet(device):
         pl.semaphore_signal(barrier, inc=1, device_id=device, device_id_type=MESH)
 
+    distant = [*range(nd - 1, 0, -2), *range(nd - 2, 0, -2), 0]
+    others = [(a, b) for a in distant for b in range(ns - 1, -1, -1) if a or b]
+
+    def each_other(body):
+        if len(others) > 15:
+            over(1, peers, lambda k: body(any_peer(k)))
+            return
+        for a, b in others:
+            body({"dp": lax.rem(d + a, nd), "seq": lax.rem(q + b, ns)})
+
+    each_other(greet)
     greet(sibling)
-    over(1, peers, lambda k: greet(any_peer(k)))
     over(1, ns, lambda k: greet({"section": other, **seq_peer(k)}))
     over(1, nd, lambda k: greet({"section": other, **dp_peer(k)}))
 
@@ -251,14 +269,14 @@
             r.bnb[ph, me, 4 + c : 5 + c, :] = lower[:, c * LANES : (c + 1) * LANES]
         r.bnb[ph, me, 8:9, :] = count_row
 
-    def to_all(ph, k):
+    def to_all(ph, device):
         block = r.bnb.at[ph, me]
-        return remote(block, block, r.bn_send.at[ph], r.bn_recv.at[ph], any_peer(k))
+        return remote(block, block, r.bn_send.at[ph], r.bn_recv.at[ph], device)
 
     def send_all(ph):
         blocks = r.bnb.at[ph, pl.ds(0, peers - 1)]
         whole = remote(blocks, blocks, r.bn_send.at[ph], r.bn_recv.at[ph], sibling)
-        begin(("all", ph), lambda: over(1, peers, lambda k: to_all(ph, k).start()), whole)
+        begin(("all", ph), lambda: each_other(lambda device: to_all(ph, device).start()), whole)
 
     def wait_all(ph):
         arrive(("all", ph))
@@ -437,51 +455,63 @@
         average = r.stat[b, 0:1, :]
         slope = r.stat[b, 1:2, :] * gain
 
-        def tile(rows, carry):
+        def tile(rows, _):
             x = r.act[b, rows, :].astype(F32)
             scaled = (wide(r.live[rows, :]) * ((x - average) * slope + bias)).astype(BF16)
             r.scaled[b, rows, :] = scaled
-            u = mm(scaled, r.win[b]) * scale_row
+            yield
+            u = mm(scaled, r.win[b])
+            yield
+            u = u * scale_row
             for c in range(4):
                 r.u[b, c, rows, :] = u[:, c * LANES : (c + 1) * LANES]
-            return carry
-
-        row_tiles(tile, 0)
-
-    def forward_out(b, finish, init):
+
+        skewed(tile, [])
+
+    def forward_out(b, finish, sums):
         skip = r.prm[b, 2:3, :]
-        value_bias, gate_bias = r.prm[b, 3:4, :], r.prm[b, 4:5, :]
-
-        def tile(rows, carry):
+        value_bias, half_gate_bias = r.prm[b, 3:4, :], 0.5 * r.prm[b, 4:5, :]
+
+        def tile(rows, sums):
             readout = jnp.concatenate([r.st[b, c, rows, :] for c in range(4)], axis=1).astype(BF16)
             r.readout[b, rows, :] = readout
-            mixed = mm(readout, r.wout[b]) + skip * r.scaled[b, rows, :].astype(F32)
+            through = mm(readout, r.wout[b])
+            yield
+            mixed = through + skip * r.scaled[b, rows, :].astype(F32)
             square = mixed * mixed
-            t = jnp.tanh(ROOT * mixed * (1.0 + CUBE * square))
+            t = jnp.tanh(mixed * (ROOT + (ROOT * CUBE) * square))
             half = 0.5 + 0.5 * t
-            active = (mixed * half).astype(BF16)
+            wide_active = mixed * half
+            active = wide_active.astype(BF16)
             r.active[b, rows, :] = active
-            r.slope[b, rows, :] = half + (0.5 * ROOT) * mixed * (1.0 - t * t) * (1.0 + (3.0 * CUBE) * square)
+            r.slope[b, rows, :] = half + wide_active * ((1.0 - t) * (ROOT + (3.0 * ROOT * CUBE) * square))
+            yield
             gated = mm(active, r.wglu[b])
-            gate = 0.5 + 0.5 * jnp.tanh(0.5 * (gated[:, D:] + gate_bias))
+            yield
+            gate = 0.5 + 0.5 * jnp.tanh(0.5 * gated[:, D:] + half_gate_bias)
             product = (gated[:, :D] + value_bias) * gate
             live = wide(r.live[rows, :])
             result = (r.act[b, rows, :].astype(F32) + live * product).astype(BF16)
             r.act[b + 1, rows, :] = result
-            return finish(rows, live, gate, product * (1.0 - gate), result, carry)
-
-        return row_tiles(tile, init)
-
-    def back_tile(b, rows, outer, gate, steep, carry):
+            yield from finish(rows, live, gate, product * (1.0 - gate), result, sums)
+
+        return skewed(tile, sums)
+
+    def back_tile(b, rows, outer, gate, steep, sums):
         grad_gated = jnp.concatenate([outer * gate, outer * steep], axis=1).astype(BF16)
         r.gg[rows, :] = grad_gated
-        grad_mixed = (r.slope[b, rows, :] * mm_t(grad_gated, r.wglu[b])).astype(BF16)
+        sums[1] = sums[1] + column_sum(grad_gated.astype(F32))
+        yield
+        grad_active = mm_t(grad_gated, r.wglu[b])
+        yield
+        grad_mixed = (r.slope[b, rows, :] * grad_active).astype(BF16)
         r.gm[rows, :] = grad_mixed
+        sums[0] = sums[0] + column_sum(grad_mixed.astype(F32) * r.scaled[b, rows, :].astype(F32))
+        yield
         grad_readout = mm_t(grad_mixed, r.wout[b])
+        yield
         for c in range(4):
             r.adj[c, rows, :] = grad_readout[:, c * LANES : (c + 1) * LANES]
-        by_skip = column_sum(grad_mixed.astype(F32) * r.scaled[b, rows, :].astype(F32))
-        return carry[0] + by_skip, carry[1] + column_sum(grad_gated.astype(F32))
 
     def normed(b, rows):
         return (r.act[b, rows, :].astype(F32) - r.stat[b, 0:1, :]) * r.stat[b, 1:2, :]
@@ -499,14 +529,16 @@
     def back_in(b):
         skip = r.prm[b, 2:3, :]
 
-        def tile(rows, carry):
-            grad_scaled = skip * r.gm[rows, :].astype(F32) + mm_t(projected_grads[b][rows, :], r.win[b])
-            masked = wide(r.live[rows, :]) * grad_scaled
+        def tile(rows, sums):
+            into = mm_t(projected_grads[b][rows, :], r.win[b])
+            yield
+            masked = wide(r.live[rows, :]) * (skip * r.gm[rows, :].astype(F32) + into)
             r.slope[b, rows, :] = masked
-            return carry[0] + column_sum(masked * normed(b, rows)), carry[1] + column_sum(masked)
+            sums[0] = sums[0] + column_sum(masked * normed(b, rows))
+            sums[1] = sums[1] + column_sum(masked)
 
         zero = jnp.zeros((1, D), F32)
-        return row_tiles(tile, (zero, zero))
+        return skewed(tile, [zero, zero])
 
     def back_norm(ph, b):
         wait_all(ph)
@@ -781,12 +813,13 @@
     starts = carry(0, r.u.at[0], ahead0, False, nothing)
     fill_states(0, starts, ahead0, False)
 
-    def finish_one(rows, live, gate, steep, result, carry):
+    def finish_one(rows, live, gate, steep, result, sums):
         r.gate[rows, :] = gate
         r.steep[rows, :] = steep
-        return carry + column_sum(result.astype(F32))
-
-    norm_sums(1, forward_out(0, finish_one, zero_row))
+        sums[0] = sums[0] + column_sum(result.astype(F32))
+        yield
+
+    norm_sums(1, forward_out(0, finish_one, [zero_row])[0])
     send_all(1)
     in_time(r.act.at[1], r.leave.at[0])
     norm_merge(1)
@@ -794,11 +827,11 @@
     starts = carry(1, r.u.at[1], ahead1, True, nothing)
     fill_states(1, starts, ahead1, True)
 
-    def finish_two(rows, live, gate, steep, result, carry):
-        return back_tile(1, rows, live * r.cotv[rows, :].astype(F32), gate, steep, carry)
+    def finish_two(rows, live, gate, steep, result, sums):
+        return back_tile(1, rows, live * r.cotv[rows, :].astype(F32), gate, steep, sums)
 
     wide_zero = jnp.zeros((1, 2 * D), F32)
-    by_skip, by_bias = forward_out(1, finish_two, (zero_row, wide_zero))
+    by_skip, by_bias = forward_out(1, finish_two, [zero_row, wide_zero])
 
     keep_act = pltpu.make_async_copy(r.leave.at[s], r.act_out.at[s], r.local.at[5])
     give_act = remote(r.leave.at[other], r.act_out.at[s], r.far_send.at[4], r.far_recv.at[4], sibling)
@@ -821,14 +854,14 @@
     go("norm two")
     slope, by_bias_total, by_gain_total = back_norm(2, 1)
 
-    def through(rows, carry):
+    def through(rows, sums):
         live = wide(r.live[rows, :])
         upstream = r.cotv[rows, :].astype(F32)
         grad = source_grad(1, rows, upstream, live, slope, by_bias_total, by_gain_total).astype(BF16)
         r.ig[rows, :] = grad
-        return back_tile(0, rows, live * grad.astype(F32), r.gate[rows, :], r.steep[rows, :], carry)
-
-    by_skip, by_bias = row_tiles(through, (zero_row, wide_zero))
+        yield from back_tile(0, rows, live * grad.astype(F32), r.gate[rows, :], r.steep[rows, :], sums)
+
+    by_skip, by_bias = skewed(through, [zero_row, wide_zero])
     go("through")
 
     def next_pieces():
@@ -1008,7 +1041,7 @@
         out_specs=[in_any if name in any_out else in_vmem for name in outs],
         scratch_shapes=list(scratch.values()),
         compiler_params=pltpu.CompilerParams(
-            collective_id=0, has_side_effects=True, vmem_limit_bytes=60 * 2**20
+            collective_id=0, has_side_effects=True, vmem_limit_bytes=61 * 2**20
         ),
     )(
         inputs.reshape(MICRO, tokens, D),

time: 98.7 us -> 95.6 us (0.969)
  Pallas kernels: 97.5 us -> 94.4 us
    pallas_call x1, Pallas kernels: 90.3 us -> 87.2 us  [body(): pl.pallas_call(functools.partial(kernel, ns, nd, per, span, names), out_s...]
where the time goes in v3:
time: 95.6 us; the launch traced here: 95.3 us
  Pallas kernels  94.4 us (99%)
    pallas_call x1, Pallas kernels, body(): pl.pallas_call(functools.partial(kernel, ns, nd, per, span, names), out_s...  87.2 us
    pallas_call x1, Pallas kernels, body(): pl.pallas_call(functools.partial(results_kernel, tokens), out_shape=[jax....  7.21 us

profile of v3, /device:TPU:0, one launch (start us, length us, event | category | flops | bytes accessed | tf_op | source)
XLA Modules:
  0.0 95.3 jit_solution(15152703017015199370)
XLA Ops:
  0.6 87.2 %shard_map.203 = (bf16[2,1024,512]{2,1,0:T(8,128)(2,1)}, bf16[2,1024,512]{2,1,0:T(8,128)(2,1)}, bf16[8192,128]{1,0:T(8,128)(2,1)}, f32[8,512]{1,0:T(8,128)}) custom-call(bf16[2,1024,512]{2,1,0:T(8,128)(2,1)} %refs_0_.1, bf16[2,1024,512]{2,1,0:T(8,128)(2,1)} %refs_1_.1, s32[2,1024]{1,0:T(2,128)} %refs_2_.1, f32[1,512]{1,0:T(1,128)} %refs_3_.1, ...), custom_call_target="tpu_custom_call" | custom-call | tf_op jit(solution)/shard_map/pallas_call | solution.py:1037
  87.9 7.2 %shard_map.204 = (bf16[2,1024,512]{2,1,0:T(8,128)(2,1)}, f32[2,1024,512]{2,1,0:T(8,128)}, f32[512,1024]{1,0:T(8,128)}, f32[512,512]{1,0:T(8,128)}, f32[512,512]{...) custom-call(bf16[2,1024,512]{2,1,0:T(8,128)(2,1)} %get-tuple-element, ...), custom_call_target="tpu_custom_call" | custom-call | tf_op jit(solution)/shard_map/pallas_call | solution.py:1064

commit v4 on v3

--- a/solution.py
+++ b/solution.py
@@ -42,7 +42,7 @@
     "filled one": (3, 2, 9),
     "norm one": (0, 102, 1, 8, 3, 2, 6, 5),
     "last": (8, 1, 9, 0, 6, 201),
-    "end": (4, 0, 5, 4, 3, 1, 2, 0, 5, 2, 4, 1, 202, 4, 9, 3, 5),
+    "end": (4, 0, 5, 4, 3, 1, 2, 0, 5, 2, 4, 1, 202, 4, 203, 204, 9, 3, 5),
 }
 ROOT = math.sqrt(2.0 / math.pi)
 CUBE = 0.044715
@@ -206,6 +206,22 @@
 
     load_x = pltpu.make_async_copy(r.x.at[s], r.act.at[0], r.local.at[0])
     load_x.start()
+    load_small = [
+        pltpu.make_async_copy(src, dst, r.local.at[8 + i])
+        for i, (src, dst) in enumerate(
+            (
+                (r.mask, r.mask_v),
+                (r.nu, r.nu_v),
+                (r.theta, r.theta_v),
+                (r.gain, r.gain_v),
+                (r.bias, r.bias_v),
+                (r.skip, r.skip_v),
+                (r.bglu, r.bglu_v),
+            )
+        )
+    ]
+    for copy in load_small:
+        copy.start()
     load_cot = pltpu.make_async_copy(r.cot.at[s], r.cotv, r.local.at[1])
     weights = ((r.w_in, r.win), (r.w_out, r.wout), (r.w_glu, r.wglu))
     load_w = [
@@ -214,9 +230,11 @@
     for copy in load_w:
         copy.start()
     load_cot.start()
-
-    rate = jnp.exp(r.nu[...])
-    phase = jnp.exp(r.theta[...])
+    for copy in load_small:
+        copy.wait()
+
+    rate = jnp.exp(r.nu_v[...])
+    phase = jnp.exp(r.theta_v[...])
     size = jnp.exp(-rate)
     decay_re = size * jnp.cos(phase)
     decay_im = size * jnp.sin(phase)
@@ -226,11 +244,11 @@
         - double / 2.0 * (1.0 - double / 3.0 * (1.0 - double / 4.0 * (1.0 - double / 5.0 * (1.0 - double / 6.0))))
     )
     scale = jnp.sqrt(scale_sq)
-    r.prm[s, 0:1, :] = r.gain[...]
-    r.prm[s, 1:2, :] = r.bias[...]
-    r.prm[s, 2:3, :] = r.skip[...]
-    r.prm[s, 3:4, :] = r.bglu[:, :D]
-    r.prm[s, 4:5, :] = r.bglu[:, D:]
+    r.prm[s, 0:1, :] = r.gain_v[...]
+    r.prm[s, 1:2, :] = r.bias_v[...]
+    r.prm[s, 2:3, :] = r.skip_v[...]
+    r.prm[s, 3:4, :] = r.bglu_v[:, :D]
+    r.prm[s, 4:5, :] = r.bglu_v[:, D:]
     r.prm[s, 5:6, :] = jnp.concatenate([decay_re, decay_im], axis=1)
     r.prm[s, 6:7, :] = jnp.concatenate([scale, scale], axis=1)
     r.prm[s, 7:8, :] = jnp.zeros((1, D), F32)
@@ -240,7 +258,7 @@
     token = (row & -ROWS) + (row & (EIGHT - 1)) * SEG + ((row & (ROWS - 1)) >> (EIGHT.bit_length() - 1))
     live = jnp.zeros((tokens, LANES), F32)
     for i in range(per):
-        here = jnp.sum(r.mask[pl.ds(s * per + i, 1), :], axis=1, keepdims=True)
+        here = jnp.sum(r.mask_v[pl.ds(s * per + i, 1), :], axis=1, keepdims=True)
         live = jnp.where((token >= i * span) & (token < i * span + here), 1.0, live)
         count = count + here.astype(F32)
     r.live[...] = live
@@ -781,7 +799,24 @@
         vec_three(0)
         alone("vec", remote(r.vec_tot.at[other], r.vec_far, r.far_send.at[6], r.far_recv.at[6], sibling))
 
-    vec_steps = (lambda: vec_two(1), lambda: vec_two(0), vec_last)
+    keep_small = pltpu.make_async_copy(r.small_v, r.small, r.local.at[7])
+
+    def small_out():
+        arrive("vec")
+        total = r.vec_tot[s] + r.vec_far[...]
+        r.small_v[0:5, :] = total[0:5]
+        grad_re, grad_im = total[5:6, :STATES], total[5:6, STATES:]
+        grad_rate = total[6:7, :STATES] * jnp.exp(-double) / scale_sq - (grad_re * decay_re + grad_im * decay_im)
+        r.small_v[5:6, :STATES] = grad_rate * rate
+        r.small_v[5:6, STATES:] = (grad_im * decay_re - grad_re * decay_im) * phase
+        r.small_v[6:8, :] = jnp.zeros((2, D), F32)
+        keep_small.start()
+
+    def let_go():
+        for key in [key for key in leaving if key not in arriving]:
+            leave(key)
+
+    vec_steps = (lambda: vec_two(1), lambda: vec_two(0), vec_last, small_out, let_go)
 
     arrive("prm")
     for i in range(3):
@@ -897,16 +932,8 @@
     go("end")
     while not all([one.step() is True for one in sums_of]):
         pass
-    arrive("vec")
-    total = r.vec_tot[s] + r.vec_far[...]
-    r.small[0:5, :] = total[0:5]
-    grad_re, grad_im = total[5:6, :STATES], total[5:6, STATES:]
-    grad_rate = total[6:7, :STATES] * jnp.exp(-double) / scale_sq - (grad_re * decay_re + grad_im * decay_im)
-    r.small[5:6, :STATES] = grad_rate * rate
-    r.small[5:6, STATES:] = (grad_im * decay_re - grad_re * decay_im) * phase
-    r.small[6:8, :] = jnp.zeros((2, D), F32)
-
     keep_ig.wait()
+    keep_small.wait()
     for one in results:
         one.finish()
     end_all()
@@ -914,22 +941,17 @@
 
 def results_kernel(
     tokens, act, ig, grads, small, o_act, o_ig, o_glu, o_out, o_in, o_gain, o_bias, o_nu, o_theta, o_skip, o_bglu,
-    act_v, ig_v, ig_f, grads_v, grads_f, act_sem, ig_sem, grad_sem,
+    act_v, ig_v, ig_f, grads_v, grads_f, small_v, gain_v, bias_v, nu_v, theta_v, skip_v, bglu_v,
+    act_sem, ig_sem, grad_sem, small_sem,
 ):
     copy = pltpu.make_async_copy
     act_in = [copy(act.at[i], act_v.at[i], act_sem.at[i, 0]) for i in range(MICRO)]
     ig_in = [copy(ig.at[i], ig_v.at[i], ig_sem.at[i, 0]) for i in range(MICRO)]
     parts = [pl.ds(GRAD_AT[i], GRAD_ROWS[i]) for i in (GLU, OUT, IN)]
     grads_in = [copy(grads.at[parts[i]], grads_v.at[parts[i]], grad_sem.at[i, 0]) for i in (GLU, OUT, IN)]
-    for one in ig_in + grads_in + act_in:
+    small_in = copy(small, small_v, small_sem.at[0])
+    for one in [small_in] + ig_in + grads_in + act_in:
         one.start()
-    o_gain[...] = small[0:1, :]
-    o_bias[...] = small[1:2, :]
-    o_skip[...] = small[2:3, :]
-    o_bglu[:, :D] = small[3:4, :]
-    o_bglu[:, D:] = small[4:5, :]
-    o_nu[...] = small[5:6, :STATES]
-    o_theta[...] = small[5:6, STATES:]
     out = []
 
     def leave(src, dst, sem):
@@ -946,6 +968,17 @@
 
         lax.fori_loop(0, tokens // 64, tile, 0)
         leave(ig_f.at[i], o_ig.at[i], ig_sem.at[i, 1])
+    small_in.wait()
+    gain_v[...] = small_v[0:1, :]
+    bias_v[...] = small_v[1:2, :]
+    skip_v[...] = small_v[2:3, :]
+    bglu_v[:, :D] = small_v[3:4, :]
+    bglu_v[:, D:] = small_v[4:5, :]
+    nu_v[...] = small_v[5:6, :STATES]
+    theta_v[...] = small_v[5:6, STATES:]
+    small_out = ((gain_v, o_gain), (bias_v, o_bias), (nu_v, o_nu), (theta_v, o_theta), (skip_v, o_skip), (bglu_v, o_bglu))
+    for i, (src, dst) in enumerate(small_out):
+        leave(src, dst, small_sem.at[1 + i])
     for i, dst in ((GLU, o_glu), (OUT, o_out), (IN, o_in)):
         grads_in[i].wait()
         for c in range(GRAD_ROWS[i] // D):
@@ -968,14 +1001,12 @@
     dma = pltpu.SemaphoreType.DMA
     vmem = pltpu.VMEM
     names_in = ["x", "cot", "mask", "gain", "bias", "nu", "theta", "skip", "bglu", "w_in", "w_out", "w_glu"]
-    any_in = {"x", "cot", "w_in", "w_out", "w_glu"}
     outs = {
         "act_out": jax.ShapeDtypeStruct((MICRO, tokens, D), BF16),
         "ig_out": jax.ShapeDtypeStruct((MICRO, tokens, D), BF16),
         "grads": jax.ShapeDtypeStruct((ALL_ROWS, LANES), BF16),
         "small": jax.ShapeDtypeStruct((8, D), F32),
     }
-    any_out = {"act_out", "ig_out", "grads"}
     half = ALL_ROWS // 2
     scratch = {
         "act": vmem((3, tokens, D), BF16),
@@ -1012,7 +1043,15 @@
         "vec_b": vmem((2, nd, 8, D), F32),
         "vec_tot": vmem((2, 8, D), F32),
         "vec_far": vmem((8, D), F32),
-        "local": dma((7,)),
+        "mask_v": vmem(mask.shape, jnp.int32),
+        "nu_v": vmem((1, STATES), F32),
+        "theta_v": vmem((1, STATES), F32),
+        "gain_v": vmem((1, D), F32),
+        "bias_v": vmem((1, D), F32),
+        "skip_v": vmem((1, D), F32),
+        "bglu_v": vmem((1, 2 * D), F32),
+        "small_v": vmem((8, D), F32),
+        "local": dma((15,)),
         "own": dma((len(FLAT),)),
         "far_send": dma((7,)),
         "far_recv": dma((7,)),
@@ -1032,13 +1071,12 @@
         "vb_recv": dma((2,)),
     }
     in_any = pl.BlockSpec(memory_space=pl.ANY)
-    in_vmem = pl.BlockSpec(memory_space=pltpu.VMEM)
     names = names_in + list(outs) + list(scratch)
     act, ig, grads, small = pl.pallas_call(
         functools.partial(kernel, ns, nd, per, span, names),
         out_shape=list(outs.values()),
-        in_specs=[in_any if name in any_in else in_vmem for name in names_in],
-        out_specs=[in_any if name in any_out else in_vmem for name in outs],
+        in_specs=[in_any] * len(names_in),
+        out_specs=[in_any] * len(outs),
         scratch_shapes=list(scratch.values()),
         compiler_params=pltpu.CompilerParams(
             collective_id=0, has_side_effects=True, vmem_limit_bytes=61 * 2**20
@@ -1064,17 +1102,20 @@
     act, ig, d_glu, d_out, d_in, d_gain, d_bias, d_nu, d_theta, d_skip, d_bglu = pl.pallas_call(
         functools.partial(results_kernel, tokens),
         out_shape=[jax.ShapeDtypeStruct(*x) for x in big_out] + [jax.ShapeDtypeStruct(x, F32) for x in wide_out],
-        in_specs=[in_any] * 3 + [in_vmem],
-        out_specs=[in_any] * 5 + [in_vmem] * 6,
+        in_specs=[in_any] * 4,
+        out_specs=[in_any] * 11,
         scratch_shapes=[
             vmem((MICRO, tokens, D), BF16),
             vmem((MICRO, tokens, D), BF16),
             vmem((MICRO, tokens, D), F32),
             vmem((ALL_ROWS, LANES), BF16),
             vmem((D, ALL_ROWS // 4), F32),
+            vmem((8, D), F32),
+            *[vmem(x, F32) for x in wide_out],
             dma((2, 2)),
             dma((2, 2)),
             dma((3, 2)),
+            dma((7,)),
         ],
         compiler_params=pltpu.CompilerParams(vmem_limit_bytes=60 * 2**20),
     )(act, ig, grads, small)

time: 95.6 us -> 93.2 us (0.975)
  Pallas kernels: 94.4 us -> 92.3 us
    pallas_call x1, Pallas kernels: 7.21 us -> 5.98 us  [body(): pl.pallas_call(functools.partial(results_kernel, tokens), out_shape=[jax....]
    pallas_call x1, Pallas kernels: 87.2 us -> 86.3 us  [body(): pl.pallas_call(functools.partial(kernel, ns, nd, per, span, names), out_s...]
where the time goes in v4:
time: 93.2 us; the launch traced here: 93.1 us
  Pallas kernels  92.3 us (99%)
    pallas_call x1, Pallas kernels, body(): pl.pallas_call(functools.partial(kernel, ns, nd, per, span, names), out_s...  86.3 us
    pallas_call x1, Pallas kernels, body(): pl.pallas_call(functools.partial(results_kernel, tokens), out_shape=[jax....  5.98 us

profile of v4, /device:TPU:0, one launch (start us, length us, event | category | flops | bytes accessed | tf_op | source)
XLA Modules:
  0.0 93.1 jit_solution(16623034217961560034)
XLA Ops:
  0.6 86.3 %shard_map.203 = (bf16[2,1024,512]{2,1,0:T(8,128)(2,1)}, bf16[2,1024,512]{2,1,0:T(8,128)(2,1)}, bf16[8192,128]{1,0:T(8,128)(2,1)}, f32[8,512]{1,0:T(8,128)}) custom-call(bf16[2,1024,512]{2,1,0:T(8,128)(2,1)} %refs_0_.1, bf16[2,1024,512]{2,1,0:T(8,128)(2,1)} %refs_1_.1, s32[2,1024]{1,0:T(2,128)} %refs_2_.1, f32[1,512]{1,0:T(1,128)} %refs_3_.1, ...), custom_call_target="tpu_custom_call" | custom-call | tf_op jit(solution)/shard_map/pallas_call | solution.py:1075
  86.9 6.0 %shard_map.204 = (bf16[2,1024,512]{2,1,0:T(8,128)(2,1)}, f32[2,1024,512]{2,1,0:T(8,128)}, f32[512,1024]{1,0:T(8,128)}, f32[512,512]{1,0:T(8,128)}, f32[512,512]{...) custom-call(bf16[2,1024,512]{2,1,0:T(8,128)(2,1)} %get-tuple-element, ...), custom_call_target="tpu_custom_call" | custom-call | tf_op jit(solution)/shard_map/pallas_call | solution.py:1102

commit v5 on v4

--- a/solution.py
+++ b/solution.py
@@ -24,25 +24,25 @@
 SD = ("seq", "dp")
 DS = ("dp", "seq")
 PARTS = (
-    ((0, 1536, SD), (1536, 1536, SD), (3072, 1024, DS),),
-    ((0, 1024, SD), (1024, 1024, DS),),
-    ((0, 2048, SD),),
-    ((0, 4096, SD),),
+    ((0, 2560, SD), (2560, 1536, DS),),
     ((0, 2048, SD),),
     ((0, 1536, SD), (1536, 512, DS),),
+    ((0, 2048, SD), (2048, 2048, SD),),
+    ((0, 2048, SD),),
+    ((0, 2048, SD),),
 )
 FLAT = tuple((n, *part) for n, parts in enumerate(PARTS) for part in parts)
 DEPTH = max(len(part[-1]) for part in FLAT)
 PLAN = {
     "carry two": (104, 103, 7),
     "filled two": (),
-    "norm two": (105, 6, 7, 8, 9),
+    "norm two": (5, 105, 7, 6, 8),
     "through": (7,),
-    "carry one": (200, 100, 6, 7, 101, 8),
-    "filled one": (3, 2, 9),
-    "norm one": (0, 102, 1, 8, 3, 2, 6, 5),
-    "last": (8, 1, 9, 0, 6, 201),
-    "end": (4, 0, 5, 4, 3, 1, 2, 0, 5, 2, 4, 1, 202, 4, 203, 204, 9, 3, 5),
+    "carry one": (200, 101, 5, 7, 6, 8, 2, 100, 5),
+    "filled one": (0, 1, 8, 5),
+    "norm one": (2, 102, 4, 6, 1, 3, 0, 1, 8),
+    "last": (201,),
+    "end": (4, 2, 6, 3, 4, 0, 2, 202, 3, 1, 203, 204, 0, 3, 4),
 }
 ROOT = math.sqrt(2.0 / math.pi)
 CUBE = 0.044715
@@ -149,9 +149,11 @@
     arriving = {}
     leaving = {}
 
-    def begin(key, start, whole):
+    def begin(key, start, whole, later=False):
         start()
-        arriving[key] = leaving[key] = whole
+        arriving[key] = whole
+        if not later:
+            leaving[key] = whole
 
     def arrive(key):
         arriving.pop(key).wait_recv()
@@ -165,8 +167,8 @@
         for key in list(leaving):
             leave(key)
 
-    def alone(key, copy):
-        begin(key, copy.start, copy)
+    def alone(key, copy, later=False):
+        begin(key, copy.start, copy, later)
 
     def row_tiles(body, init):
         def step(i, carry):
@@ -617,7 +619,7 @@
         def to_core(self):
             size = self.sizes[0]
             src = r.dw.at[self.b, pl.ds(pl.multiple_of(self.at + other * size, 16), size)]
-            return remote(src, r.sec.at[self.b, self.rows(0, size)], r.core_send.at[self.n], r.core_recv.at[self.n], sibling)
+            return remote(src, r.sec.at[self.b, self.rows(0, size)], r.send.at[self.n], r.core_recv.at[self.n], sibling)
 
         def slot(self, level, index):
             start, size = self.slots[level]
@@ -631,11 +633,11 @@
                 size = self.sizes[level + 1]
                 src = r.half.at[self.b, self.rows(self.offsets[level] + lax.rem(index + k, count) * size, size)]
             dst = r.slots.at[self.slot(level, index)]
-            return remote(src, dst, r.rs_send.at[self.n, level], r.rs_recv.at[self.n, level], peer(k))
+            return remote(src, dst, r.send.at[self.n], r.rs_recv.at[self.n, level], peer(k))
 
         def gather(self, level, k):
             block = r.gat.at[self.b, self.rows(self.offsets[level + 1], self.sizes[level + 1])]
-            return remote(block, block, r.ag_send.at[self.n, level], r.ag_recv.at[self.n, level], self.axes[level][2](k))
+            return remote(block, block, r.send.at[self.n], r.ag_recv.at[self.n, level], self.axes[level][2](k))
 
         def place(self):
             return pl.ds(pl.multiple_of(self.at + s * self.sizes[0] + self.offsets[1], 16), self.sizes[1])
@@ -647,7 +649,7 @@
 
         def results_whole(self, parts):
             rows = r.grads.at[pl.ds(0, parts * self.sizes[1])]
-            return remote(rows, rows, r.ag_send.at[self.n, 0], r.ag_recv.at[self.n, 0], sibling)
+            return remote(rows, rows, r.send.at[self.n], r.ag_recv.at[self.n, 0], sibling)
 
         def own(self):
             src = r.gat.at[self.b, self.rows(self.offsets[1], self.sizes[1])]
@@ -686,17 +688,17 @@
                 r.slots[self.slot(level, self.axes[level][1]), :] = r.half[self.b, here, :]
             start, size = self.slots[level]
             rows = r.slots.at[pl.ds(self.slot_base + start, (self.axes[level][0] - 1) * size)]
-            whole = remote(rows, rows, r.rs_send.at[self.n, level], r.rs_recv.at[self.n, level], sibling)
-            begin((self.n, "scatter", level), lambda: self.each(level, lambda k: self.scatter(level, k).start()), whole)
+            whole = remote(rows, rows, r.send.at[self.n], r.rs_recv.at[self.n, level], sibling)
+            begin((self.n, "scatter", level), lambda: self.each(level, lambda k: self.scatter(level, k).start()), whole, True)
 
         def share(self, level):
             count, _, peer = self.axes[level]
             if level:
                 rows = r.gat.at[self.b, pl.ds(self.base, (count - 1) * self.sizes[level + 1])]
-                whole = remote(rows, rows, r.ag_send.at[self.n, level], r.ag_recv.at[self.n, level], sibling)
-                begin((self.n, "gather", level), lambda: self.each(level, lambda k: self.gather(level, k).start()), whole)
+                whole = remote(rows, rows, r.send.at[self.n], r.ag_recv.at[self.n, level], sibling)
+                begin((self.n, "gather", level), lambda: self.each(level, lambda k: self.gather(level, k).start()), whole, True)
                 return
-            self.each(0, lambda k: self.result(peer(k), r.ag_send.at[self.n, 0]).start())
+            self.each(0, lambda k: self.result(peer(k), r.send.at[self.n]).start())
 
             @pl.when(s == self.b)
             def _():
@@ -720,13 +722,19 @@
             def _():
                 self.across().wait_send()
 
-            if count > 1:
-                self.results_whole(count - 1).wait_send()
+            sent = self.sizes[0] + (count - 1) * self.sizes[1]
+            top = len(self.axes) - (2 if self.spread else 1)
+            for level, (n, _, _) in enumerate(self.axes):
+                sent += (n - 1) * self.slots[level][1]
+                if 0 < level <= top:
+                    sent += (n - 1) * self.sizes[level + 1]
+            rows = r.dw.at[self.b, pl.ds(0, sent)]
+            remote(rows, rows, r.send.at[self.n], r.core_recv.at[self.n], sibling).wait_send()
 
         def plan(self):
             depth = len(self.axes)
             top = depth - 2 if self.spread else depth - 1
-            yield alone((self.n, "core"), self.to_core())
+            yield alone((self.n, "core"), self.to_core(), True)
             self.first()
             yield self.send(0)
             for level in range(1, depth):
@@ -1059,11 +1067,9 @@
         "bn_recv": dma((4,)),
         "sc_send": dma((4,)),
         "sc_recv": dma((4,)),
-        "core_send": dma((len(FLAT),)),
+        "send": dma((len(FLAT),)),
         "core_recv": dma((len(FLAT),)),
-        "rs_send": dma((len(FLAT), DEPTH)),
         "rs_recv": dma((len(FLAT), DEPTH)),
-        "ag_send": dma((len(FLAT), DEPTH)),
         "ag_recv": dma((len(FLAT), DEPTH)),
         "va_send": dma((2,)),
         "va_recv": dma((2,)),

time: 93.2 us -> 92.3 us (level)
  Pallas kernels: 92.3 us -> 91.3 us
where the time goes in v5:
time: 92.3 us; the launch traced here: 92.2 us
  Pallas kernels  91.3 us (99%)
    pallas_call x1, Pallas kernels, body(): pl.pallas_call(functools.partial(kernel, ns, nd, per, span, names), out_s...  85.4 us
    pallas_call x1, Pallas kernels, body(): pl.pallas_call(functools.partial(results_kernel, tokens), out_shape=[jax....  5.98 us

profile of v5, /device:TPU:0, one launch (start us, length us, event | category | flops | bytes accessed | tf_op | source)
XLA Modules:
  0.0 92.2 jit_solution(12172060289545041569)
XLA Ops:
  0.6 85.4 %shard_map.203 = (bf16[2,1024,512]{2,1,0:T(8,128)(2,1)}, bf16[2,1024,512]{2,1,0:T(8,128)(2,1)}, bf16[8192,128]{1,0:T(8,128)(2,1)}, f32[8,512]{1,0:T(8,128)}) custom-call(bf16[2,1024,512]{2,1,0:T(8,128)(2,1)} %refs_0_.1, bf16[2,1024,512]{2,1,0:T(8,128)(2,1)} %refs_1_.1, s32[2,1024]{1,0:T(2,128)} %refs_2_.1, f32[1,512]{1,0:T(1,128)} %refs_3_.1, ...), custom_call_target="tpu_custom_call" | custom-call | tf_op jit(solution)/shard_map/pallas_call | solution.py:1081
  86.0 6.0 %shard_map.204 = (bf16[2,1024,512]{2,1,0:T(8,128)(2,1)}, f32[2,1024,512]{2,1,0:T(8,128)}, f32[512,1024]{1,0:T(8,128)}, f32[512,512]{1,0:T(8,128)}, f32[512,512]{...) custom-call(bf16[2,1024,512]{2,1,0:T(8,128)(2,1)} %get-tuple-element, ...), custom_call_target="tpu_custom_call" | custom-call | tf_op jit(solution)/shard_map/pallas_call | solution.py:1108

commit v6 on v5

--- a/solution.py
+++ b/solution.py
@@ -287,14 +287,17 @@
         for c in range(4):
             r.bnb[ph, me, c : c + 1, :] = upper[:, c * LANES : (c + 1) * LANES]
             r.bnb[ph, me, 4 + c : 5 + c, :] = lower[:, c * LANES : (c + 1) * LANES]
-        r.bnb[ph, me, 8:9, :] = count_row
+        if ph == 0:
+            r.bnb[ph, me, 8:9, :] = count_row
 
     def to_all(ph, device):
-        block = r.bnb.at[ph, me]
+        block = r.bnb.at[ph, me] if ph == 0 else r.bnb.at[ph, me, pl.ds(0, 8)]
         return remote(block, block, r.bn_send.at[ph], r.bn_recv.at[ph], device)
 
     def send_all(ph):
         blocks = r.bnb.at[ph, pl.ds(0, peers - 1)]
+        if ph > 0:
+            blocks = r.bnb.at[ph, pl.ds(0, peers - 1), pl.ds(0, 8)]
         whole = remote(blocks, blocks, r.bn_send.at[ph], r.bn_recv.at[ph], sibling)
         begin(("all", ph), lambda: each_other(lambda device: to_all(ph, device).start()), whole)
 
@@ -307,8 +310,8 @@
 
     def norm_merge(b):
         wait_all(b)
-        got = r.bnb[b]
-        means, spreads, counts = got[:, 0:4, :], got[:, 4:8, :], got[:, 8:9, :]
+        got, counts = r.bnb[b, :, 0:8, :], r.bnb[0, :, 8:9, :]
+        means, spreads = got[:, 0:4, :], got[:, 4:8, :]
         valid = jnp.sum(counts, axis=0)
         mean = jnp.sum(counts * means, axis=0) / valid
         apart = means - mean[None]
@@ -562,7 +565,7 @@
 
     def back_norm(ph, b):
         wait_all(ph)
-        got = jnp.sum(r.bnb[ph], axis=0)
+        got = jnp.sum(r.bnb[ph, :, 0:8, :], axis=0)
         gain_total, bias_total = as_row(got[0:4]), as_row(got[4:8])
         r.vec_tot[b, 0:1, :] = gain_total
         r.vec_tot[b, 1:2, :] = bias_total

time: 92.3 us -> 91.9 us (level)
  no operation moved by 1% of the time
where the time goes in v6:
time: 91.9 us; the launch traced here: 91.8 us
  Pallas kernels  91 us (99%)
    pallas_call x1, Pallas kernels, body(): pl.pallas_call(functools.partial(kernel, ns, nd, per, span, names), out_s...  85 us
    pallas_call x1, Pallas kernels, body(): pl.pallas_call(functools.partial(results_kernel, tokens), out_shape=[jax....  5.98 us

profile of v6, /device:TPU:0, one launch (start us, length us, event | category | flops | bytes accessed | tf_op | source)
XLA Modules:
  0.0 91.8 jit_solution(13819004568557258551)
XLA Ops:
  0.6 85.0 %shard_map.203 = (bf16[2,1024,512]{2,1,0:T(8,128)(2,1)}, bf16[2,1024,512]{2,1,0:T(8,128)(2,1)}, bf16[8192,128]{1,0:T(8,128)(2,1)}, f32[8,512]{1,0:T(8,128)}) custom-call(bf16[2,1024,512]{2,1,0:T(8,128)(2,1)} %refs_0_.1, bf16[2,1024,512]{2,1,0:T(8,128)(2,1)} %refs_1_.1, s32[2,1024]{1,0:T(2,128)} %refs_2_.1, f32[1,512]{1,0:T(1,128)} %refs_3_.1, ...), custom_call_target="tpu_custom_call" | custom-call | tf_op jit(solution)/shard_map/pallas_call | solution.py:1084
  85.6 6.0 %shard_map.204 = (bf16[2,1024,512]{2,1,0:T(8,128)(2,1)}, f32[2,1024,512]{2,1,0:T(8,128)}, f32[512,1024]{1,0:T(8,128)}, f32[512,512]{1,0:T(8,128)}, f32[512,512]{...) custom-call(bf16[2,1024,512]{2,1,0:T(8,128)(2,1)} %get-tuple-element, ...), custom_call_target="tpu_custom_call" | custom-call | tf_op jit(solution)/shard_map/pallas_call | solution.py:1111
